TPU v7x, 128 devices: a whole 4x4x4 slice. The times are simulated.
128 devices in a mesh: row: 16 (over x, y), grp: 8 (over z, core).
Axes of the slice: x: 4, y: 4, z: 4, core: 2. Of those that a mesh axis runs over, the one named last changes fastest.
Arguments:
- node_feat: bfloat16 [131072, 256], P(('row', 'grp')), may hold values from -6 to 6
- edge_feat: bfloat16 [524288, 256], P(('row', 'grp')), may hold values from -6 to 6
- senders: int32 [524288], P(('row', 'grp')), may hold values from 0 to 1279, as said below
- receivers: int32 [524288], P(('row', 'grp')), may hold values from 0 to 1023
- edge_count: int32 [128], P(('row', 'grp')), may hold values from 1024 to 4096, as said below
- halo_index: int32 [128, 8, 32], P(('row', 'grp')), may hold values from 0 to 1023
- coarse_target: int32 [131072], P(('row', 'grp')), may hold values from 0 to 511, as said below
- restrict_weight: bfloat16 [131072], P(('row', 'grp')), may hold values from 0.25 to 1
- prolong_weight: bfloat16 [131072], P(('row', 'grp')), may hold values from 0.5 to 1.5
- edge_in: bfloat16 [768, 256], replicated, may hold values from -0.21875 to 0.21875
- edge_bias: bfloat16 [256], replicated, may hold values from -3 to 3
- edge_out: bfloat16 [256, 256], replicated, may hold values from -0.375 to 0.375
- node_in: bfloat16 [512, 256], replicated, may hold values from -0.25 to 0.25
- node_bias: bfloat16 [256], replicated, may hold values from -3 to 3
- node_out: bfloat16 [256, 256], replicated, may hold values from -0.375 to 0.375
- coarse_in: bfloat16 [256, 256], replicated, may hold values from -0.375 to 0.375
- coarse_bias: bfloat16 [256], replicated, may hold values from -3 to 3
- coarse_out: bfloat16 [256, 256], replicated, may hold values from -0.375 to 0.375
- prolong: bfloat16 [256, 256], replicated, may hold values from -0.375 to 0.375
- grad_nodes: bfloat16 [131072, 256], P(('row', 'grp')), may hold values from -6 to 6
- grad_edges: bfloat16 [524288, 256], P(('row', 'grp')), may hold values from -6 to 6
Outputs:
- node_result: float32 [131072, 256], P(('row', 'grp'))
- edge_new: float32 [524288, 256], P(('row', 'grp'))
- d_node_feat: float32 [131072, 256], P(('row', 'grp'))
- d_edge_feat: float32 [524288, 256], P(('row', 'grp'))
- d_edge_in: float32 [768, 256], replicated
- d_edge_bias: float32 [256], replicated
- d_edge_out: float32 [256, 256], replicated
- d_node_in: float32 [512, 256], replicated
- d_node_bias: float32 [256], replicated
- d_node_out: float32 [256, 256], replicated
- d_coarse_in: float32 [256, 256], replicated
- d_coarse_bias: float32 [256], replicated
- d_coarse_out: float32 [256, 256], replicated
- d_prolong: float32 [256, 256], replicated
Inputs may be any that keep to these rules, and one draw needn't show every extreme that they name: `edge_count`: edge slots in use in each partition's padded block of 4096; some partition is full in every draw. Most senders are local rows; the others are halo slots. `coarse_target`: most fine nodes of a partition map into the 64 coarse rows that its grp index owns.
All inputs are finite; a program needn't handle non-finite values.
Results may differ from a plain program's by a relative error of at most 0.017.
Values may be sent and summed in bfloat16 or wider, within the bound.
A program may use at most 128 MiB of HBM per device.

v0:
```python
import jax
import jax.numpy as jnp
from jax import lax
from jax.sharding import PartitionSpec as P

NC_DEV = 64


OFFSETS = ((-1, -1), (-1, 0), (-1, 1), (0, -1), (0, 1), (1, -1), (1, 0), (1, 1))


def from_behind(value, axis, steps):
    count = lax.axis_size(axis)
    initial, last = (max(0, -steps), min(count, count - steps))
    return lax.ppermute(value, axis, [(source, source + steps) for source in range(initial, last)])


def as_sent(value):
    return jax.tree.map(lambda a: a.astype(jnp.bfloat16) if a.dtype == jnp.float32 else a, value)


def matmul(a, b):
    return jnp.dot(a, b, preferred_element_type=jnp.float32)


def contract_rows(a, b):
    return lax.dot_general(a, b, (((0,), (0,)), ((), ())), preferred_element_type=jnp.float32)


def silu_slope(u):
    sg = jax.nn.sigmoid(u)
    return sg * (1.0 + u * (1.0 - sg))


def coarse_forward(coarse, coarse_in, coarse_bias, coarse_out):
    pre_coarse = matmul(coarse.astype(jnp.bfloat16), coarse_in) + coarse_bias.astype(jnp.float32)
    hid_coarse = jax.nn.silu(pre_coarse).astype(jnp.bfloat16)
    return (coarse + matmul(hid_coarse, coarse_out), pre_coarse, hid_coarse)


def coarse_backward(coarse, pre_coarse, hid_coarse, q_rows, summed, coarse_in, coarse_out, prolong):
    summed_b = summed.astype(jnp.bfloat16)
    grad_cn = matmul(summed_b, prolong.T)
    grad_cnb = grad_cn.astype(jnp.bfloat16)
    grad_uc = matmul(grad_cnb, coarse_out.T) * silu_slope(pre_coarse)
    grad_ucb = grad_uc.astype(jnp.bfloat16)
    grad_c = grad_cn + matmul(grad_ucb, coarse_in.T)
    grads = (
        contract_rows(coarse.astype(jnp.bfloat16), grad_ucb),
        jnp.sum(grad_uc, axis=0),
        contract_rows(hid_coarse, grad_cnb),
        contract_rows(q_rows, summed_b),
    )
    return (grad_c, grads)


def body(
    node_feat,
    edge_feat,
    senders,
    receivers,
    edge_count,
    halo_index,
    coarse_target,
    restrict_weight,
    prolong_weight,
    edge_in,
    edge_bias,
    edge_out,
    node_in,
    node_bias,
    node_out,
    coarse_in,
    coarse_bias,
    coarse_out,
    prolong,
    grad_nodes,
    grad_edges,
):
    bf = jnp.bfloat16
    f32 = jnp.float32
    width = node_feat.shape[1]
    nodes = node_feat.shape[0]
    edges = edge_feat.shape[0]
    slot_rows = halo_index.shape[2]
    own_rows = node_feat[halo_index[0]]
    sectioned = [own_rows[d] for d in range(8)]
    for row_step in (-1, 1):
        chosen = [d for d in range(8) if OFFSETS[d][0] == row_step]
        arrived = from_behind(jnp.stack([sectioned[d] for d in chosen]), "row", row_step)
        for place, d in enumerate(chosen):
            sectioned[d] = arrived[place]
    for group_step in (-1, 1):
        chosen = [d for d in range(8) if OFFSETS[d][1] == group_step]
        arrived = from_behind(jnp.stack([sectioned[d] for d in chosen]), "grp", group_step)
        for place, d in enumerate(chosen):
            sectioned[d] = arrived[place]
    incoming = jnp.stack(sectioned)
    extended = jnp.concatenate([node_feat, incoming.reshape(-1, width)], axis=0)
    sent_rows = extended[senders]
    recv_rows = node_feat[receivers]
    valid = (jnp.arange(edges, dtype=jnp.int32) < edge_count[0]).astype(f32)[:, None]
    a_edge, a_send, a_recv = (edge_in[:width], edge_in[width : 2 * width], edge_in[2 * width :])
    c_node, c_agg = (node_in[:width], node_in[width:])
    pre_edge = (
        matmul(edge_feat, a_edge)
        + matmul(sent_rows, a_send)
        + matmul(recv_rows, a_recv)
        + edge_bias.astype(f32)
    )
    hid_edge = jax.nn.silu(pre_edge).astype(bf)
    edge_new = edge_feat.astype(f32) + valid * matmul(hid_edge, edge_out)
    recv_onehot = (receivers[:, None] == jnp.arange(nodes, dtype=jnp.int32)[None, :]).astype(bf)
    agg = contract_rows(recv_onehot, (valid * edge_new).astype(bf)).astype(bf)
    pre_node = matmul(node_feat, c_node) + matmul(agg, c_agg) + node_bias.astype(f32)
    hid_node = jax.nn.silu(pre_node).astype(bf)
    updated = node_feat.astype(f32) + matmul(hid_node, node_out)
    group_rows = lax.axis_size("grp") * NC_DEV
    target_onehot = (
        coarse_target[:, None] == jnp.arange(group_rows, dtype=jnp.int32)[None, :]
    ).astype(bf)
    weighted = target_onehot * restrict_weight[:, None]
    partial_sum = contract_rows(weighted, updated.astype(bf))
    pweight = prolong_weight.astype(f32)[:, None]
    rweight = restrict_weight.astype(f32)[:, None]
    grad_z = grad_nodes.astype(f32)
    scaled = (pweight * grad_z).astype(bf)
    summed_part = contract_rows(target_onehot, scaled)
    coarse = lax.psum_scatter(partial_sum, "grp", scatter_dimension=0, tiled=True)
    coarse_new, pre_coarse, hid_coarse = coarse_forward(coarse, coarse_in, coarse_bias, coarse_out)
    q_own = coarse_new.astype(bf)
    q_rows = lax.all_gather(q_own, "grp", axis=0, tiled=True)
    node_result = updated + pweight * matmul(q_rows[coarse_target], prolong)
    summed = lax.psum_scatter(summed_part, "grp", scatter_dimension=0, tiled=True)
    grad_c, coarse_grads = coarse_backward(
        coarse, pre_coarse, hid_coarse, q_own, summed, coarse_in, coarse_out, prolong
    )
    grad_rows = lax.all_gather(grad_c.astype(bf), "grp", axis=0, tiled=True)
    grad_y = grad_z + rweight * grad_rows[coarse_target].astype(f32)
    grad_yb = grad_y.astype(bf)
    grad_un = matmul(grad_yb, node_out.T) * silu_slope(pre_node)
    grad_unb = grad_un.astype(bf)
    node_out_grad = contract_rows(hid_node, grad_yb)
    node_in_grad = jnp.concatenate(
        [contract_rows(node_feat, grad_unb), contract_rows(agg, grad_unb)], axis=0
    )
    node_bias_grad = jnp.sum(grad_un, axis=0)
    grad_agg = matmul(grad_unb, c_agg.T).astype(bf)
    grad_en = grad_edges.astype(f32) + valid * grad_agg[receivers].astype(f32)
    grad_mb = (valid * grad_en).astype(bf)
    grad_ue = matmul(grad_mb, edge_out.T) * silu_slope(pre_edge)
    grad_ueb = grad_ue.astype(bf)
    edge_out_grad = contract_rows(hid_edge, grad_mb)
    edge_in_grad = jnp.concatenate(
        [
            contract_rows(edge_feat, grad_ueb),
            contract_rows(sent_rows, grad_ueb),
            contract_rows(recv_rows, grad_ueb),
        ],
        axis=0,
    )
    edge_bias_grad = jnp.sum(grad_ue, axis=0)
    d_edge_feat = grad_en + matmul(grad_ueb, a_edge.T)
    grad_send = matmul(grad_ueb, a_send.T).astype(bf)
    grad_recv = matmul(grad_ueb, a_recv.T).astype(bf)
    send_onehot = (
        senders[:, None] == jnp.arange(extended.shape[0], dtype=jnp.int32)[None, :]
    ).astype(bf)
    grad_ext = contract_rows(send_onehot, grad_send)
    d_node_feat = (
        grad_y
        + matmul(grad_unb, c_node.T)
        + contract_rows(recv_onehot, grad_recv)
        + grad_ext[:nodes]
    )
    halo_back = grad_ext[nodes:].reshape(8, slot_rows, width)
    sectioned = [halo_back[d] for d in range(8)]
    for group_step in (-1, 1):
        chosen = [d for d in range(8) if OFFSETS[d][1] == group_step]
        arrived = from_behind(
            jnp.stack([sectioned[d] for d in chosen]).astype(jnp.bfloat16), "grp", -group_step
        ).astype(jnp.float32)
        for place, d in enumerate(chosen):
            sectioned[d] = arrived[place]
    for row_step in (-1, 1):
        chosen = [d for d in range(8) if OFFSETS[d][0] == row_step]
        arrived = from_behind(as_sent(jnp.stack([sectioned[d] for d in chosen])), "row", -row_step)
        for place, d in enumerate(chosen):
            sectioned[d] = arrived[place]
    returned = jnp.stack(sectioned)
    d_node_feat = d_node_feat.at[halo_index[0].reshape(-1)].add(returned.reshape(-1, width))
    other_grads = (
        edge_in_grad,
        edge_bias_grad,
        edge_out_grad,
        node_in_grad,
        node_bias_grad,
        node_out_grad,
    )
    all_grads = lax.psum(other_grads + coarse_grads, ("row", "grp"))
    return (node_result, edge_new, d_node_feat, d_edge_feat) + tuple(all_grads)


def solution(mesh):
    in_specs = (
        P(("row", "grp"), None),
        P(("row", "grp"), None),
        P(("row", "grp")),
        P(("row", "grp")),
        P(("row", "grp")),
        P(("row", "grp"), None, None),
        P(("row", "grp")),
        P(("row", "grp")),
        P(("row", "grp")),
        P(),
        P(),
        P(),
        P(),
        P(),
        P(),
        P(),
        P(),
        P(),
        P(),
        P(("row", "grp"), None),
        P(("row", "grp"), None),
    )
    out_specs = (
        P(("row", "grp"), None),
        P(("row", "grp"), None),
        P(("row", "grp"), None),
        P(("row", "grp"), None),
        P(),
        P(),
        P(),
        P(),
        P(),
        P(),
        P(),
        P(),
        P(),
        P(),
    )
    return jax.shard_map(body, mesh=mesh, in_specs=in_specs, out_specs=out_specs, check_vma=False)
```

profile of v0, /device:TPU:1, one launch (start us, length us, event | category | flops | bytes accessed | tf_op | source)
XLA Modules:
  0.0 381.4 jit_solution(15947362162064501223)
XLA Ops:
  10.2 4.2 %collective-permute-start.1 = (bf16[3,32,256]{2,1,0:T(8,128)(2,1)S(1)}, bf16[3,32,256]{2,1,0:T(8,128)(2,1)S(1)}, u32[]{:S(2)}, u32[]{:S(2)}) collective-permute-start(bf16[3,32,256]{2,1,0:T(8,128)(2,1)S(1)} %bitcast.82), channel_id=1, source_target_pairs={{0,8},{8,16},{16,24},{24,32},{32,40},{40,48},{48,56},{56,64},{64,7... | collective-permute-start | bytes 147464 | tf_op jit(solution)/shard_map/ppermute | solution.py:15
  17.0 2.9 fusion.8
  21.2 3.6 fusion.40
  24.9 2.9 collective-permute-start.2
  33.6 17.0 %gather_fusion.2 = bf16[4096,256]{1,0:T(8,128)(2,1)} fusion(bf16[1024,256]{1,0:T(8,128)(2,1)S(1)} %copy-done.1, s32[4096]{0:T(1024)S(1)} %get-tuple-element.61), kind=kCustom, calls=%fused_computation.2 | custom fusion | bytes 4210688 | tf_op jit(solution)/shard_map/gather | solution.py:101
  51.9 18.3 %gather_fusion.1 = bf16[4096,256]{1,0:T(8,128)(2,1)} fusion(bf16[1280,256]{1,0:T(8,128)(2,1)S(1)} %pad_maximum_fusion.1, s32[4096]{0:T(1024)} %get-tuple-element.60), kind=kCustom, calls=%fused_computation.1 | custom fusion | bytes 4210688 | tf_op jit(solution)/shard_map/gather | solution.py:100
  70.2 3.7 convolution_add_fusion.2
  73.9 4.2 %multiply_convert_fusion.2 = (bf16[4096,256]{1,0:T(8,128)(2,1)S(1)}, f32[4096,256]{1,0:T(8,128)}) fusion(f32[256]{0:T(256)S(1)} %copy-done.70, f32[4096,256]{1,0:T(8,128)S(1)} %convolution_add_fusion.2, bf16[4096,256]{1,0:T(8,128)(2,1)S(1)} %copy-done.11, bf16[768,256]{1,0:T(8,128)(2,1)} %param.30), kind=kOutput, calls=%fused_computation.27 | convolution fusion | flops 544210944 | bytes 12715008 | tf_op jit(solution)/shard_map/dot_general | solution.py:23
  80.9 5.6 %fusion.15 = bf16[1024,256]{1,0:T(8,128)(2,1)S(1)} fusion(f32[4096,256]{1,0:T(8,128)S(1)} %fusion.6, f32[4096]{0:T(1024)S(1)} %fusion.59, s32[4096]{0:T(1024)S(1)} %copy-done.53), kind=kOutput, calls=%fused_computation.44 | convolution fusion | flops 2154037248 | bytes 4751360 | tf_op jit(solution)/shard_map/dot_general | solution.py:27
  92.6 29.5 %reduce-scatter.3.cloned.1.call-done = f32[64,256]{1,0:T(8,128)} async-done(((f32[512,256]{1,0:T(8,128)}), f32[64,256]{1,0:T(8,128)}) %reduce-scatter.3.cloned.1.call-update) | async-done | bytes 65552 | tf_op jit(solution)/shard_map/reduce_scatter | solution.py:129
  124.5 16.4 %all_gather.7 = bf16[512,256]{1,0:T(8,128)(2,1)S(1)} all-gather(bf16[64,256]{1,0:T(8,128)(2,1)S(1)} %fusion.17), channel_id=1, replica_groups=mesh['row'=16,'grp'=8] {'grp'}, dimensions={0}, use_global_device_ids=true | all-gather | bytes 294912 | tf_op jit(solution)/shard_map/all_gather | solution.py:138
  140.9 3.9 %gather_fusion.4 = bf16[1024,256]{1,0:T(8,128)(2,1)S(1)} fusion(bf16[512,256]{1,0:T(8,128)(2,1)S(1)} %all_gather.7, s32[1024]{0:T(1024)S(1)} %fusion.60), kind=kCustom, calls=%fused_computation.4 | custom fusion | bytes 1052672 | tf_op jit(solution)/shard_map/gather | solution.py:139
  146.1 2.5 fusion.67
  150.4 17.0 %gather_fusion.5 = bf16[4096,256]{1,0:T(8,128)(2,1)} fusion(bf16[1024,256]{1,0:T(8,128)(2,1)S(1)} %convolution_convert_fusion.2, s32[4096]{0:T(1024)S(1)} %copy-done.43), kind=kCustom, calls=%fused_computation.5 | custom fusion | bytes 4210688 | tf_op jit(solution)/shard_map/gather | solution.py:149
  167.4 5.2 %fusion.65 = f32[256,256]{1,0:T(8,128)} fusion(bf16[4096,256]{1,0:T(8,128)(2,1)} %copy-done.10, bf16[4096,256]{1,0:T(8,128)(2,1)} %gather_fusion.5, bf16[4096,256]{1,0:T(8,128)(2,1)} %param.41, f32[4096]{0:T(1024)S(1)} %fusion.59), kind=kOutput, calls=%fused_computation.134 | convolution fusion | flops 543162368 | bytes 6569984 | tf_op jit(solution)/shard_map/dot_general | solution.py:27
  172.7 3.8 fusion.66
  182.3 2.8 convolution_add_fusion
  187.2 6.1 %fusion.1 = f32[1024,256]{1,0:T(8,128)} fusion(s32[4096]{0:T(1024)S(1)} %copy-done.54, bf16[4096,256]{1,0:T(8,128)(2,1)S(1)} %get-tuple-element.25, bf16[768,256]{1,0:T(8,128)(2,1)S(1)} %copy-done.18), kind=kOutput, calls=%fused_computation.10 | convolution fusion | flops 2689597440 | bytes 3293184 | tf_op jit(solution)/shard_map/dot_general | solution.py:27
  193.3 9.2 %fusion.73 = (bf16[1280,256]{1,0:T(8,128)(2,1)S(1)}, f32[1280,256]{1,0:T(8,128)}) fusion(s32[4096]{0:T(1024)S(1)} %copy-done.56, bf16[4096,256]{1,0:T(8,128)(2,1)} %convolution_convert_fusion.clone.1.clone.5), kind=kOutput, calls=%fused_computation.142 | convolution fusion | flops 2689925120 | bytes 4079616 | tf_op jit(solution)/shard_map/dot_general | solution.py:27
  213.9 12.8 %all_gather.6 = bf16[512,256]{1,0:T(8,128)(2,1)S(1)} all-gather(bf16[64,256]{1,0:T(8,128)(2,1)S(1)} %fusion.16), channel_id=1, replica_groups=mesh['row'=16,'grp'=8] {'grp'}, dimensions={0}, use_global_device_ids=true | all-gather | bytes 294912 | tf_op jit(solution)/shard_map/all_gather | solution.py:132
  226.8 3.9 %gather_fusion.3 = bf16[1024,256]{1,0:T(8,128)(2,1)S(1)} fusion(bf16[512,256]{1,0:T(8,128)(2,1)S(1)} %all_gather.6, s32[1024]{0:T(1024)S(1)} %copy-done.48), kind=kCustom, calls=%fused_computation.3 | custom fusion | bytes 1052672 | tf_op jit(solution)/shard_map/gather | solution.py:133
  230.8 3.1 collective-permute-start.6
  236.5 67.9 %all-reduce = (f32[256]{0:T(256)}, f32[256]{0:T(256)}, f32[256]{0:T(256)}) all-reduce(f32[256]{0:T(256)S(1)} %copy-done.63, f32[256]{0:T(256)S(1)} %copy-done.62, f32[256]{0:T(256)S(1)} %copy-done.61), channel_id=1, replica_groups=mesh['row'=16,'grp'=8] {'row','grp'}, use_global_device_ids=true, to_apply=%region_5.6 | all-reduce | flops 768 | bytes 6144 | tf_op jit(solution)/shard_map/psum | solution.py:200
  307.0 60.1 %all-reduce.4.cloned.1.call-done = (f32[768,256]{1,0:T(8,128)}, f32[256,256]{1,0:T(8,128)}, f32[512,256]{1,0:T(8,128)}, f32[256,256]{1,0:T(8,128)}, f32[256,256]...) async-done(((f32[768,256]{1,0:T(8,128)}, f32[256,256]{1,0:T(8,128)}, f32[512,256]{1,0:T(8,128)}, f32[256,256]{1,0:T(8,128)}, f32[256,256]{1,0:T(8,128)}, ...) | async-done | bytes 2621456 | tf_op jit(solution)/shard_map/psum | solution.py:200
  (234 shorter events, 59.1 us)
Async XLA Ops:
  7.2 72.3 %copy-start = (bf16[256,256]{1,0:T(8,128)(2,1)S(1)}, bf16[256,256]{1,0:T(8,128)(2,1)}, u32[]{:S(2)}) copy-start(bf16[256,256]{1,0:T(8,128)(2,1)} %param.32) | copy-start | bytes 393220
  7.2 84.4 %reduce-scatter.5.cloned.1.call-start = ((), (), s32[]{:S(2)}) async-start(), calls=%async_computation.3 | async-start | bytes 589824 | tf_op jit(solution)/shard_map/reduce_scatter | solution.py:134
  10.2 14.7 %collective-permute-start.1 = (bf16[3,32,256]{2,1,0:T(8,128)(2,1)S(1)}, bf16[3,32,256]{2,1,0:T(8,128)(2,1)S(1)}, u32[]{:S(2)}, u32[]{:S(2)}) collective-permute-start(bf16[3,32,256]{2,1,0:T(8,128)(2,1)S(1)} %bitcast.82), channel_id=1, source_target_pairs={{0,8},{8,16},{16,24},{24,32},{32,40},{40,48},{48,56},{56,64},{64,7... | collective-permute-start | bytes 147464 | tf_op jit(solution)/shard_map/ppermute | solution.py:15
  14.4 10.5 %collective-permute-start = (bf16[3,32,256]{2,1,0:T(8,128)(2,1)S(1)}, bf16[3,32,256]{2,1,0:T(8,128)(2,1)S(1)}, u32[]{:S(2)}, u32[]{:S(2)}) collective-permute-start(bf16[3,32,256]{2,1,0:T(8,128)(2,1)S(1)} %bitcast.81), channel_id=1, source_target_pairs={{8,0},{16,8},{24,16},{32,24},{40,32},{48,40},{56,48},{64,56},{72,6... | collective-permute-start | bytes 147464 | tf_op jit(solution)/shard_map/ppermute | solution.py:15
  19.9 102.2 %reduce-scatter.3.cloned.1.call-start = ((), (), s32[]{:S(2)}) async-start(), calls=%async_computation.2 | async-start | bytes 589824 | tf_op jit(solution)/shard_map/reduce_scatter | solution.py:129
  24.9 6.2 %collective-permute-start.2 = (bf16[3,32,256]{2,1,0:T(8,128)(2,1)S(1)}, bf16[3,32,256]{2,1,0:T(8,128)(2,1)S(1)}, u32[]{:S(2)}, u32[]{:S(2)}) collective-permute-start(bf16[3,32,256]{2,1,0:T(8,128)(2,1)S(1)} %pad_maximum_fusion.4), channel_id=1, source_target_pairs={{1,0},{2,1},{3,2},{4,3},{5,4},{6,5},{7,6},{9,8},{10,9},{11,10},{12... | collective-permute-start | bytes 147464 | tf_op jit(solution)/shard_map/ppermute | solution.py:15
  28.4 22.2 %copy-start.42 = (s32[4096]{0:T(1024)}, s32[4096]{0:T(1024)S(1)}, u32[]{:S(2)}) copy-start(s32[4096]{0:T(1024)S(1)} %get-tuple-element.61) | copy-start | bytes 49156
  31.1 20.7 %collective-permute-start.3 = (bf16[3,32,256]{2,1,0:T(8,128)(2,1)S(1)}, bf16[3,32,256]{2,1,0:T(8,128)(2,1)S(1)}, u32[]{:S(2)}, u32[]{:S(2)}) collective-permute-start(bf16[3,32,256]{2,1,0:T(8,128)(2,1)S(1)} %pad_maximum_fusion.5), channel_id=1, source_target_pairs={{0,1},{1,2},{2,3},{3,4},{4,5},{5,6},{6,7},{8,9},{9,10},{10,11},{11... | collective-permute-start | bytes 147464 | tf_op jit(solution)/shard_map/ppermute | solution.py:15
  33.6 17.1 %copy-start.66 = (bf16[256]{0:T(256)(128)(2,1)S(1)}, bf16[256]{0:T(256)(128)(2,1)}, u32[]{:S(2)}) copy-start(bf16[256]{0:T(256)(128)(2,1)} %param.31) | copy-start | bytes 1540
  33.6 17.6 %copy-start.67 = (bf16[256]{0:T(256)(128)(2,1)S(1)}, bf16[256]{0:T(256)(128)(2,1)}, u32[]{:S(2)}) copy-start(bf16[256]{0:T(256)(128)(2,1)} %param.34) | copy-start | bytes 1540
  89.2 32.9 %copy-start.25 = (bf16[256,256]{1,0:T(8,128)(2,1)S(1)}, bf16[256,256]{1,0:T(8,128)(2,1)}, u32[]{:S(2)}) copy-start(bf16[256,256]{1,0:T(8,128)(2,1)} %param.36) | copy-start | bytes 393220
  89.2 33.9 %copy-start.64 = (bf16[256,256]{1,0:T(8,128)(2,1)S(1)}, bf16[256,256]{1,0:T(8,128)(2,1)}, u32[]{:S(2)}) copy-start(bf16[256,256]{1,0:T(8,128)(2,1)} %param.38) | copy-start | bytes 393220
  90.9 276.2 %all-reduce.4.cloned.1.call-start = ((), (), s32[]{:S(2)}) async-start(), calls=%async_computation.4 | async-start | bytes 5242880 | tf_op jit(solution)/shard_map/psum | solution.py:200
  91.0 53.9 %copy-start.57 = (f32[1024]{0:T(1024)}, f32[1024]{0:T(1024)S(1)}, u32[]{:S(2)}) copy-start(f32[1024]{0:T(1024)S(1)} %convert_element_type.138) | copy-start | bytes 12292
  91.6 53.3 %copy-start.47 = (s32[1024]{0:T(1024)}, s32[1024]{0:T(1024)S(1)}, u32[]{:S(2)}) copy-start(s32[1024]{0:T(1024)S(1)} %fusion.60) | copy-start | bytes 12292
  92.6 31.3 %copy-start.22 = (f32[64,256]{1,0:T(8,128)}, f32[64,256]{1,0:T(8,128)S(1)}, u32[]{:S(2)}) copy-start(f32[64,256]{1,0:T(8,128)S(1)} %fusion.55) | copy-start | bytes 196612
  193.3 15.7 %copy-start.34 = (f32[256,256]{1,0:T(8,128)S(1)}, f32[256,256]{1,0:T(8,128)}, u32[]{:S(2)}) copy-start(f32[256,256]{1,0:T(8,128)} %fusion.77) | copy-start | bytes 786436
  193.3 15.7 %copy-start.35 = (f32[256,256]{1,0:T(8,128)S(1)}, f32[256,256]{1,0:T(8,128)}, u32[]{:S(2)}) copy-start(f32[256,256]{1,0:T(8,128)} %fusion.78) | copy-start | bytes 786436
  193.3 15.7 %copy-start.36 = (f32[256,256]{1,0:T(8,128)S(1)}, f32[256,256]{1,0:T(8,128)}, u32[]{:S(2)}) copy-start(f32[256,256]{1,0:T(8,128)} %convolution_bitcast_fusion.1) | copy-start | bytes 786436
  203.2 27.6 %collective-permute-start.4 = (bf16[3,32,256]{2,1,0:T(8,128)(2,1)}, bf16[3,32,256]{2,1,0:T(8,128)(2,1)S(1)}, u32[]{:S(2)}, u32[]{:S(2)}) collective-permute-start(bf16[3,32,256]{2,1,0:T(8,128)(2,1)} %pad_maximum_fusion.6), channel_id=1, source_target_pairs={{0,1},{1,2},{2,3},{3,4},{4,5},{5,6},{6,7},{8,9},{9,10},{10,11},{11... | collective-permute-start | bytes 147464 | tf_op jit(solution)/shard_map/ppermute | solution.py:15
  205.7 25.1 %collective-permute-start.5 = (bf16[3,32,256]{2,1,0:T(8,128)(2,1)}, bf16[3,32,256]{2,1,0:T(8,128)(2,1)S(1)}, u32[]{:S(2)}, u32[]{:S(2)}) collective-permute-start(bf16[3,32,256]{2,1,0:T(8,128)(2,1)} %pad_maximum_fusion.7), channel_id=1, source_target_pairs={{1,0},{2,1},{3,2},{4,3},{5,4},{6,5},{7,6},{9,8},{10,9},{11,10},{12... | collective-permute-start | bytes 147464 | tf_op jit(solution)/shard_map/ppermute | solution.py:15
  230.8 73.6 %collective-permute-start.6 = (bf16[3,32,256]{2,1,0:T(8,128)(2,1)S(1)}, bf16[3,32,256]{2,1,0:T(8,128)(2,1)S(1)}, u32[]{:S(2)}, u32[]{:S(2)}) collective-permute-start(bf16[3,32,256]{2,1,0:T(8,128)(2,1)S(1)} %pad_maximum_fusion.8), channel_id=1, source_target_pairs={{0,8},{8,16},{16,24},{24,32},{32,40},{40,48},{48,56},{56,64},{64,7... | collective-permute-start | bytes 147464 | tf_op jit(solution)/shard_map/ppermute | solution.py:15
  233.9 70.6 %collective-permute-start.7 = (bf16[3,32,256]{2,1,0:T(8,128)(2,1)S(1)}, bf16[3,32,256]{2,1,0:T(8,128)(2,1)S(1)}, u32[]{:S(2)}, u32[]{:S(2)}) collective-permute-start(bf16[3,32,256]{2,1,0:T(8,128)(2,1)S(1)} %pad_maximum_fusion.9), channel_id=1, source_target_pairs={{8,0},{16,8},{24,16},{32,24},{40,32},{48,40},{56,48},{64,56},{72,6... | collective-permute-start | bytes 147464 | tf_op jit(solution)/shard_map/ppermute | solution.py:15
  307.0 66.1 %copy-start.17 = (f32[1024,256]{1,0:T(8,128)}, f32[1024,256]{1,0:T(8,128)S(1)}, u32[]{:S(2)}) copy-start(f32[1024,256]{1,0:T(8,128)S(1)} %scatter_custom_fusion) | copy-start | bytes 3145732
  (59 other events, 289.0 us)
Sparse Core Ops, SparseCore 0:
  20.0 31.9 reduce-scatter.4
  91.0 31.0 reduce-scatter.2
  212.1 155.0 all-reduce.3
where the time goes:
time: 385 us; the launch traced here: 381 us
  blocking collectives  97.2 us (25%)
  waiting for transfers between devices  91.6 us (24%)
  local copies, waits for them, and re-layouts  74.1 us (19%)
  matrix products  74.1 us (19%)
  starting transfers between devices  19.5 us (5%)
  between operations  15.5 us (4%)
  other arithmetic  9.38 us (2%)
    psum x1, blocking collectives, body(): all_grads = lax.psum(other_grads + coarse_grads, ('row', 'grp'))  67.9 us
    psum x1, waiting for transfers between devices, body(): all_grads = lax.psum(other_grads + coarse_grads, ('row', 'grp'))  60.1 us
    dot_general x15, matrix products, contract_rows(): lax.dot_general(a, b, (((0,), (0,)), ((), ())), preferred_element_type=jn...  40.5 us
    dot_general x19, matrix products, matmul(): return jnp.dot(a, b, preferred_element_type=jnp.float32)  33.6 us
    reduce_scatter x1, waiting for transfers between devices, body(): lax.psum_scatter(partial_sum, 'grp', scatter_dimension=0, tiled=True)  29.5 us
    ppermute x8, starting transfers between devices, from_behind(): lax.ppermute(value, axis, [(source, source + steps) for source in range(i...  19.4 us
    gather x1, local copies, waits for them, and re-layouts, body(): sent_rows = extended[senders]  18.3 us
    gather x1, local copies, waits for them, and re-layouts, body(): grad_en = grad_edges.astype(f32) + valid * grad_agg[receivers].astype(f32)  17 us
  transfers between devices with their start and end apart: 11, of which 3 were waited for; matrix products, arithmetic and copies ran while one was open for 21% of the time, Pallas kernels for 0%

commit v1 on v0

v1 whole, which is shorter than its diff:
```python
import jax
import jax.numpy as jnp
from jax import lax
from jax.experimental import pallas as pl
from jax.experimental.pallas import tpu as pltpu
from jax.sharding import PartitionSpec as P

BF = jnp.bfloat16
F32 = jnp.float32
I32 = jnp.int32
MESH = pl.DeviceIdType.MESH
OFFSETS = ((-1, -1), (-1, 0), (-1, 1), (0, -1), (0, 1), (1, -1), (1, 0), (1, 1))
NR, NG = 16, 8
H = 256
NF = 1024
EF = 4096
NX = 1280
NT = NX + NF
GC = 512
NC = 64
BLK = 1024
SUB = 512
MIB = 1024 * 1024


def mm(a, b):
    return lax.dot_general(a, b, (((1,), (0,)), ((), ())), preferred_element_type=F32)


def mm_nt(a, b):
    return lax.dot_general(a, b, (((1,), (1,)), ((), ())), preferred_element_type=F32)


def mm_tn(a, b):
    return lax.dot_general(a, b, (((0,), (0,)), ((), ())), preferred_element_type=F32)


def silu_parts(u):
    sg = jax.nn.sigmoid(u)
    return u * sg, sg * (1.0 + u * (1.0 - sg))


def hot_rows(idx, lo, count, weight=None):
    parts = []
    for j in range(idx.shape[0]):
        place = lax.broadcasted_iota(I32, (count, 128), 0) + lo
        value = 1.0 if weight is None else weight[j : j + 1, :]
        parts.append(jnp.where(place == idx[j : j + 1, :], value, 0.0).astype(BF))
    return jnp.concatenate(parts, axis=1)


def hot_cols(idx_t, lo, count, weight_t=None):
    parts = []
    for j in range(idx_t.shape[1]):
        place = lax.broadcasted_iota(I32, (128, count), 1) + lo
        value = 1.0 if weight_t is None else weight_t[:, j : j + 1]
        parts.append(jnp.where(place == idx_t[:, j : j + 1], value, 0.0).astype(BF))
    return jnp.concatenate(parts, axis=0)


def halo_columns(hidx):
    wide = hidx.astype(F32)
    eye = lax.broadcasted_iota(I32, (32, 32), 0) == lax.broadcasted_iota(I32, (32, 32), 1)
    return [
        jnp.sum(jnp.where(eye, wide[d : d + 1, :], 0.0), axis=1, keepdims=True) for d in range(8)
    ]


def here():
    return lax.axis_index("row"), lax.axis_index("grp")


def shifted(r, g, dr, dg):
    return lax.rem(r + dr + NR, NR), lax.rem(g + dg + NG, NG)


def inside(r, g, dr, dg):
    rr, gg = r + dr, g + dg
    return (rr >= 0) & (rr < NR) & (gg >= 0) & (gg < NG)


def greet(r, g, steps):
    barrier = pltpu.get_barrier_semaphore()
    for dr, dg in steps:
        pl.semaphore_signal(
            barrier, inc=1, device_id=shifted(r, g, dr, dg), device_id_type=MESH
        )
    return lambda: pl.semaphore_wait(barrier, len(steps))


def over(n, fn):
    def step(k, carry):
        fn(k)
        return carry

    lax.fori_loop(1, n, step, 0)


def remote(src, dst, send, recv, place):
    return pltpu.make_async_remote_copy(
        src_ref=src, dst_ref=dst, send_sem=send, recv_sem=recv, device_id=place, device_id_type=MESH
    )


def rows(start, size):
    return pl.ds(pl.multiple_of(start * size, size), size)


GRP_STEPS = [(0, k) for k in range(1, NG)]
ROW_STEPS = [(k, 0) for k in range(1, NR)]
NEAR_STEPS = [(dr, dg) for dr, dg in OFFSETS]
HALO_PEERS = GRP_STEPS + [s for s in NEAR_STEPS if s[0] != 0]
ALL_PEERS = GRP_STEPS + ROW_STEPS + [s for s in NEAR_STEPS if s[0] != 0 and s[1] != 0]


def scatter_grp(r, g, part, land, send, recv, size):
    def copy(k):
        t = lax.rem(g + k, NG)
        return remote(part.at[rows(t, size)], land.at[k - 1], send.at[k - 1], recv.at[k - 1], (r, t))

    return copy


def halo_kernel(nf, hidx, ct, pw, gz, ein, p_out, halo_out, s_out, own, land, part, sland,
                hs, hr, ss, sr):
    r, g = here()
    ready = greet(r, g, HALO_PEERS)
    pick = jnp.concatenate(
        [
            jnp.where(lax.broadcasted_iota(I32, (32, NF), 1).astype(F32) == c, 1.0, 0.0).astype(BF)
            for c in halo_columns(hidx[...])
        ],
        axis=0,
    )
    own[...] = mm(pick, nf[...]).astype(BF)
    ready()
    halo = [
        remote(
            own.at[pl.ds(32 * d, 32)], land.at[pl.ds(32 * d, 32)], hs.at[d], hr.at[d],
            shifted(r, g, dr, dg),
        )
        for d, (dr, dg) in enumerate(OFFSETS)
    ]
    for c in halo:
        c.start()
    part[...] = mm(hot_rows(ct[...], 0, GC, pw[...].astype(F32)), gz[...]).astype(BF)
    scat = scatter_grp(r, g, part, sland, ss, sr, NC)
    over(NG, lambda k: scat(k).start())
    p_out[0:NF] = mm(nf[...], ein[H : 2 * H]).astype(BF)
    p_out[NX:] = mm(nf[...], ein[2 * H :]).astype(BF)
    for c in halo:
        c.wait()
    for d, (dr, dg) in enumerate(OFFSETS):
        got = land[32 * d : 32 * d + 32]
        halo_out[32 * d : 32 * d + 32] = jnp.where(inside(r, g, -dr, -dg), got, jnp.zeros_like(got))
    p_out[NF:NX] = mm(halo_out[...], ein[H : 2 * H]).astype(BF)
    over(NG, lambda k: scat(k).wait())
    total = part[rows(g, NC)].astype(F32)
    for k in range(NG - 1):
        total += sland[k].astype(F32)
    s_out[...] = total.astype(BF)


def mask_of(count, start, size):
    place = lax.broadcasted_iota(I32, (size, 1), 0) + start
    return jnp.where(place < count, 1.0, 0.0)


def edge_forward_kernel(count, ef, snd, rcv, ptab, ein, ebias, eout, en_out, he_out, ds_out, agg_out,
                        acc):
    step = pl.program_id(0)

    @pl.when(step == 0)
    def _():
        acc[...] = jnp.zeros_like(acc)

    snd_t = jnp.transpose(snd[...])
    rcv_t = jnp.transpose(rcv[...])
    bias = ebias[...].astype(F32)
    per = SUB // 128
    for h in range(BLK // SUB):
        at = slice(h * SUB, (h + 1) * SUB)
        lanes = slice(h * per, (h + 1) * per)
        x = ef[at]
        u = mm(x, ein[0:H]) + bias
        u += mm(hot_cols(snd_t[:, lanes], 0, NX), ptab[0:NX])
        u += mm(hot_cols(rcv_t[:, lanes], 0, NF), ptab[NX:])
        s, slope = silu_parts(u)
        he = s.astype(BF)
        he_out[at] = he
        ds_out[at] = slope.astype(BF)
        m = mask_of(count[0], step * BLK + h * SUB, SUB)
        new = x.astype(F32) + m * mm(he, eout[...])
        en_out[at] = new
        acc[...] += mm(hot_rows(rcv[lanes], 0, NF), (m * new).astype(BF))

    @pl.when(step == pl.num_programs(0) - 1)
    def _():
        agg_out[...] = acc[...].astype(BF)


def coarse_kernel(nf, agg, nin, nbias, nout, ct, rw, s_in, cin, cbias, cout, prol,
                  y_out, hn_out, dsn_out, gc_out, q_out, wc_out, cb_out,
                  part, land, gc_own, ss, sr, gs, gr):
    r, g = here()
    ready = greet(r, g, GRP_STEPS)
    un = mm(nf[...], nin[0:H]) + mm(agg[...], nin[H:]) + nbias[...].astype(F32)
    s, slope = silu_parts(un)
    hn = s.astype(BF)
    hn_out[...] = hn
    dsn_out[...] = slope.astype(BF)
    y = nf[...].astype(F32) + mm(hn, nout[...])
    y_out[...] = y
    part[...] = mm(hot_rows(ct[...], 0, GC, rw[...].astype(F32)), y.astype(BF)).astype(BF)
    ready()
    scat = scatter_grp(r, g, part, land, ss, sr, NC)
    over(NG, lambda k: scat(k).start())
    sb = s_in[...]
    gcn = mm_nt(sb, prol[...])
    gcnb = gcn.astype(BF)
    gh = mm_nt(gcnb, cout[...])
    over(NG, lambda k: scat(k).wait())
    c = part[rows(g, NC)].astype(F32)
    for k in range(NG - 1):
        c += land[k].astype(F32)
    cb = c.astype(BF)
    uc = mm(cb, cin[...]) + cbias[...].astype(F32)
    s, slope = silu_parts(uc)
    hc = s.astype(BF)
    guc = gh * slope
    gucb = guc.astype(BF)
    gc = (gcn + mm_nt(gucb, cin[...])).astype(BF)
    gc_own[...] = gc
    gc_out[rows(g, NC)] = gc

    def gather(k):
        return remote(
            gc_own, gc_out.at[rows(g, NC)], gs.at[k - 1], gr.at[k - 1], (r, lax.rem(g + k, NG))
        )

    over(NG, lambda k: gather(k).start())
    q = (c + mm(hc, cout[...])).astype(BF)
    q_out[...] = q
    wc_out[0:H] = mm_tn(cb, gucb).astype(BF)
    wc_out[H : 2 * H] = mm_tn(hc, gcnb).astype(BF)
    wc_out[2 * H :] = mm_tn(q, sb).astype(BF)
    cb_out[...] = jnp.sum(guc, axis=0, keepdims=True)
    over(NG, lambda k: gather(k).wait())


def backward_kernel(count, ef, ge, snd, rcv, he, ds, nf, agg, gz, hn, dsn, gc, ct, rw, halo,
                    ein, eout, nin, nout,
                    def_out, wl_out, wn_out, b_out, dn_out, dh_out,
                    gagg, gyn, ssum, wacc, bacc):
    step = pl.program_id(0)

    @pl.when(step == 0)
    def _():
        ssum[...] = jnp.zeros_like(ssum)
        wacc[...] = jnp.zeros_like(wacc)
        bacc[...] = jnp.zeros_like(bacc)
        table = hot_cols(jnp.transpose(ct[...]), 0, GC, jnp.transpose(rw[...].astype(F32)))
        gy = gz[...].astype(F32) + mm(table, gc[...])
        gyb = gy.astype(BF)
        gun = mm_nt(gyb, nout[...]) * dsn[...].astype(F32)
        gunb = gun.astype(BF)
        gagg[...] = mm_nt(gunb, nin[H:]).astype(BF)
        gyn[...] = gy + mm_nt(gunb, nin[0:H])
        wn_out[0:H] = mm_tn(nf[...], gunb).astype(BF)
        wn_out[H : 2 * H] = mm_tn(agg[...], gunb).astype(BF)
        wn_out[2 * H :] = mm_tn(hn[...], gyb).astype(BF)
        bacc[1:2] = jnp.sum(gun, axis=0, keepdims=True)

    rcv_t = jnp.transpose(rcv[...])
    per = SUB // 128
    for h in range(BLK // SUB):
        at = slice(h * SUB, (h + 1) * SUB)
        lanes = slice(h * per, (h + 1) * per)
        m = mask_of(count[0], step * BLK + h * SUB, SUB)
        gen = ge[at].astype(F32) + m * mm(hot_cols(rcv_t[:, lanes], 0, NF), gagg[...])
        gm = (m * gen).astype(BF)
        gue = mm_nt(gm, eout[...]) * ds[at].astype(F32)
        gueb = gue.astype(BF)
        def_out[at] = gen + mm_nt(gueb, ein[0:H])
        wacc[0:H] += mm_tn(ef[at], gueb)
        wacc[H:] += mm_tn(he[at], gm)
        bacc[0:1] += jnp.sum(gue, axis=0, keepdims=True)
        ssum[0:NX] += mm(hot_rows(snd[lanes], 0, NX), gueb)
        ssum[NX:] += mm(hot_rows(rcv[lanes], 0, NF), gueb)

    @pl.when(step == pl.num_programs(0) - 1)
    def _():
        sb = ssum[...].astype(BF)
        send_grad = mm_nt(sb[0:NX], ein[H : 2 * H])
        dh_out[...] = send_grad[NF:].astype(BF)
        dn_out[...] = gyn[...] + send_grad[0:NF] + mm_nt(sb[NX:], ein[2 * H :])
        wl_out[0:H] = wacc[0:H].astype(BF)
        wl_out[H : 2 * H] = (mm_tn(nf[...], sb[0:NF]) + mm_tn(halo[...], sb[NF:NX])).astype(BF)
        wl_out[2 * H : 3 * H] = mm_tn(nf[...], sb[NX:]).astype(BF)
        wl_out[3 * H :] = wacc[H:].astype(BF)
        b_out[...] = bacc[...]


ROWS_A, ROWS_B = 1536, 1024
WROWS = ROWS_A + ROWS_B
RA, RB = ROWS_A // NG, ROWS_B // NR


def half(p):
    return pl.ds(pl.multiple_of(lax.rem(p, 2) * 128, 128), 128)


def sum_kernel(wl, wn, wc, b_in, cb_in, dh, q_in,
               w_out, b_out, q_out, h_out,
               wbuf, a1, b1, accA, accB, a2, b2, pa, pb, gA, gB, bias0, bias1, bl1, bl2, land,
               hs, hr, qs, qr, a1s, a1r, b1s, b1r, a2s, a2r, b2s, b2r, a3s, a3r, b3s, b3r,
               a4s, a4r, b4s, b4r, c1s, c1r, c2s, c2r):
    r, g = here()
    ready = greet(r, g, ALL_PEERS)
    wbuf[0:1024] = wl[...]
    wbuf[1024:1792] = wn[...]
    wbuf[1792:2560] = wc[...]
    bias0[...] = b_in[...]
    bias0[2:3] = cb_in[...]
    ready()

    def grp(k):
        return (r, lax.rem(g + k, NG))

    def row(k):
        return (lax.rem(r + k, NR), g)

    halo = [
        remote(
            dh.at[pl.ds(32 * d, 32)], land.at[pl.ds(32 * d, 32)], hs.at[d], hr.at[d],
            shifted(r, g, -dr, -dg),
        )
        for d, (dr, dg) in enumerate(OFFSETS)
    ]
    for c in halo:
        c.start()

    def s1a(k):
        t = lax.rem(g + k, NG)
        return remote(wbuf.at[rows(t, RA)], a1.at[k - 1], a1s.at[k - 1], a1r.at[k - 1], (r, t))

    def s1b(k):
        t = lax.rem(r + k, NR)
        src = wbuf.at[pl.ds(pl.multiple_of(ROWS_A + t * RB, RB), RB)]
        return remote(src, b1.at[k - 1], b1s.at[k - 1], b1r.at[k - 1], (t, g))

    def c1(k):
        return remote(bias0, bl1.at[k - 1], c1s.at[k - 1], c1r.at[k - 1], grp(k))

    def c2(k):
        return remote(bias1, bl2.at[k - 1], c2s.at[k - 1], c2r.at[k - 1], row(k))

    def gq(k):
        return remote(q_in, q_out.at[rows(g, NC)], qs.at[k - 1], qr.at[k - 1], grp(k))

    over(NR, lambda k: s1b(k).start())
    over(NG, lambda k: s1a(k).start())
    over(NG, lambda k: c1(k).start())
    over(NG, lambda k: gq(k).start())
    q_out[rows(g, NC)] = q_in[...]

    PA, PB = RA // 8, RB // 4

    def s2a(k):
        t = lax.rem(r + k, NR)
        src = accA.at[rows(t // 2, PA), half(t)]
        return remote(src, a2.at[k - 1], a2s.at[k - 1], a2r.at[k - 1], (t, g))

    def s2b(k):
        t = lax.rem(g + k, NG)
        src = accB.at[rows(t // 2, PB), half(t)]
        return remote(src, b2.at[k - 1], b2s.at[k - 1], b2r.at[k - 1], (r, t))

    over(NR, lambda k: s1b(k).wait())
    total = wbuf[pl.ds(pl.multiple_of(ROWS_A + r * RB, RB), RB)].astype(F32)
    for k in range(NR - 1):
        total += b1[k].astype(F32)
    accB[...] = total
    over(NG, lambda k: s2b(k).start())

    over(NG, lambda k: s1a(k).wait())
    total = wbuf[rows(g, RA)].astype(F32)
    for k in range(NG - 1):
        total += a1[k].astype(F32)
    accA[...] = total
    over(NR, lambda k: s2a(k).start())

    over(NG, lambda k: c1(k).wait())
    total = bias0[...]
    for k in range(NG - 1):
        total += bl1[k]
    bias1[...] = total
    over(NR, lambda k: c2(k).start())

    def s3a(k):
        dst = gA.at[rows(r // 2, PA), half(r)]
        return remote(pa, dst, a3s.at[k - 1], a3r.at[k - 1], row(k))

    def s3b(k):
        dst = gB.at[rows(g // 2, PB), half(g)]
        return remote(pb, dst, b3s.at[k - 1], b3r.at[k - 1], grp(k))

    over(NG, lambda k: s2b(k).wait())
    total = accB[rows(g // 2, PB), half(g)]
    for k in range(NG - 1):
        total += b2[k]
    pb[...] = total
    gB[rows(g // 2, PB), half(g)] = total
    over(NG, lambda k: s3b(k).start())

    over(NR, lambda k: s2a(k).wait())
    total = accA[rows(r // 2, PA), half(r)]
    for k in range(NR - 1):
        total += a2[k]
    pa[...] = total
    gA[rows(r // 2, PA), half(r)] = total
    over(NR, lambda k: s3a(k).start())

    def s4a(k):
        at = w_out.at[rows(g, RA)]
        return remote(at, at, a4s.at[k - 1], a4r.at[k - 1], grp(k))

    def s4b(k):
        at = w_out.at[pl.ds(pl.multiple_of(ROWS_A + r * RB, RB), RB)]
        return remote(at, at, b4s.at[k - 1], b4r.at[k - 1], row(k))

    over(NG, lambda k: s3b(k).wait())
    w_out[pl.ds(pl.multiple_of(ROWS_A + r * RB, RB), RB)] = gB[...].astype(BF)
    over(NR, lambda k: s4b(k).start())

    over(NR, lambda k: s3a(k).wait())
    w_out[rows(g, RA)] = gA[...].astype(BF)
    over(NG, lambda k: s4a(k).start())

    for c in halo:
        c.wait()
    for d, (dr, dg) in enumerate(OFFSETS):
        got = land[32 * d : 32 * d + 32]
        h_out[32 * d : 32 * d + 32] = jnp.where(inside(r, g, dr, dg), got, jnp.zeros_like(got))
    over(NG, lambda k: gq(k).wait())
    over(NR, lambda k: c2(k).wait())
    total = bias1[...]
    for k in range(NR - 1):
        total += bl2[k]
    b_out[...] = total
    over(NR, lambda k: s4b(k).wait())
    over(NG, lambda k: s4a(k).wait())


def result_kernel(w, b, q, back, dn, y, ct, pw, hidx, prol,
                  nr_out, dnf_out, o_ein, o_eb, o_eout, o_nin, o_nb, o_nout, o_cin, o_cb, o_cout, o_pr):
    table = hot_cols(jnp.transpose(ct[...]), 0, GC, jnp.transpose(pw[...].astype(F32)))
    nr_out[...] = y[...] + mm(table, mm(q[...], prol[...]).astype(BF))
    pick = jnp.concatenate(
        [
            jnp.where(lax.broadcasted_iota(I32, (32, NF), 1).astype(F32) == c, 1.0, 0.0).astype(BF)
            for c in halo_columns(hidx[...])
        ],
        axis=0,
    )
    dnf_out[...] = dn[...] + mm_tn(pick, back[...])
    o_ein[...] = w[0:768].astype(F32)
    o_eout[...] = w[768:1024].astype(F32)
    o_nin[...] = w[1024:1536].astype(F32)
    o_nout[...] = w[1536:1792].astype(F32)
    o_cin[...] = w[1792:2048].astype(F32)
    o_cout[...] = w[2048:2304].astype(F32)
    o_pr[...] = w[2304:2560].astype(F32)
    o_eb[...] = b[0:1]
    o_nb[...] = b[1:2]
    o_cb[...] = b[2:3]


def body(node_feat, edge_feat, senders, receivers, edge_count, halo_index, coarse_target,
         restrict_weight, prolong_weight, edge_in, edge_bias, edge_out, node_in, node_bias, node_out,
         coarse_in, coarse_bias, coarse_out, prolong, grad_nodes, grad_edges):
    snd = senders.reshape(EF // 128, 128)
    rcv = receivers.reshape(EF // 128, 128)
    ct = coarse_target.reshape(NF // 128, 128)
    rw = restrict_weight.reshape(NF // 128, 128)
    pw = prolong_weight.reshape(NF // 128, 128)
    hidx = halo_index.reshape(8, 32)
    ebias, nbias, cbias = (v.reshape(1, H) for v in (edge_bias, node_bias, coarse_bias))

    def shape(dims, dtype=BF):
        return jax.ShapeDtypeStruct(dims, dtype)

    def sems(*sizes):
        return [pltpu.SemaphoreType.DMA((n,)) for n in sizes]

    def whole(n):
        return [pl.BlockSpec(memory_space=pltpu.VMEM)] * n

    smem = pl.BlockSpec(memory_space=pltpu.SMEM)

    def comm(ident, limit):
        return pltpu.CompilerParams(
            collective_id=ident, has_side_effects=True, vmem_limit_bytes=limit * MIB
        )

    ptab, halo, s_own = pl.pallas_call(
        halo_kernel,
        out_shape=[shape((NT, H)), shape((256, H)), shape((NC, H))],
        in_specs=whole(6),
        out_specs=whole(3),
        scratch_shapes=[
            pltpu.VMEM((256, H), BF),
            pltpu.VMEM((256, H), BF),
            pltpu.VMEM((GC, H), BF),
            pltpu.VMEM((NG - 1, NC, H), BF),
        ]
        + sems(8, 8, NG - 1, NG - 1),
        compiler_params=comm(0, 40),
        name="halo",
    )(node_feat, hidx, ct, pw, grad_nodes, edge_in)

    blocks = EF // BLK

    def by_edge(width=H):
        return pl.BlockSpec((BLK, width), lambda i: (i, 0))

    def fixed(dims):
        return pl.BlockSpec(dims, lambda i: (0, 0))

    idx_spec = pl.BlockSpec((BLK // 128, 128), lambda i: (i, 0))
    edge_new, he, ds, agg = pl.pallas_call(
        edge_forward_kernel,
        grid=(blocks,),
        out_shape=[shape((EF, H), F32), shape((EF, H)), shape((EF, H)), shape((NF, H))],
        in_specs=[
            smem, by_edge(), idx_spec, idx_spec, fixed((NT, H)), fixed((768, H)), fixed((1, H)),
            fixed((H, H)),
        ],
        out_specs=[by_edge(), by_edge(), by_edge(), fixed((NF, H))],
        scratch_shapes=[pltpu.VMEM((NF, H), F32)],
        compiler_params=pltpu.CompilerParams(
            dimension_semantics=("arbitrary",), vmem_limit_bytes=56 * MIB
        ),
        name="edge_forward",
    )(edge_count, edge_feat, snd, rcv, ptab, edge_in, ebias, edge_out)

    y, hn, dsn, gc, q, wc, cb = pl.pallas_call(
        coarse_kernel,
        out_shape=[
            shape((NF, H), F32), shape((NF, H)), shape((NF, H)), shape((GC, H)), shape((NC, H)),
            shape((768, H)), shape((1, H), F32),
        ],
        in_specs=whole(12),
        out_specs=whole(7),
        scratch_shapes=[
            pltpu.VMEM((GC, H), BF),
            pltpu.VMEM((NG - 1, NC, H), BF),
            pltpu.VMEM((NC, H), BF),
        ]
        + sems(*[NG - 1] * 4),
        compiler_params=comm(1, 40),
        name="coarse",
    )(node_feat, agg, node_in, nbias, node_out, ct, rw, s_own, coarse_in, cbias, coarse_out, prolong)

    d_edge_feat, wl, wn, bias, dn, dh = pl.pallas_call(
        backward_kernel,
        grid=(blocks,),
        out_shape=[
            shape((EF, H), F32), shape((1024, H)), shape((768, H)), shape((8, H), F32),
            shape((NF, H), F32), shape((256, H)),
        ],
        in_specs=[
            smem, by_edge(), by_edge(), idx_spec, idx_spec, by_edge(), by_edge(),
            fixed((NF, H)), fixed((NF, H)), fixed((NF, H)), fixed((NF, H)), fixed((NF, H)),
            fixed((GC, H)), fixed((8, 128)), fixed((8, 128)), fixed((256, H)),
            fixed((768, H)), fixed((H, H)), fixed((512, H)), fixed((H, H)),
        ],
        out_specs=[
            by_edge(), fixed((1024, H)), fixed((768, H)), fixed((8, H)), fixed((NF, H)), fixed((256, H)),
        ],
        scratch_shapes=[
            pltpu.VMEM((NF, H), BF),
            pltpu.VMEM((NF, H), F32),
            pltpu.VMEM((NT, H), F32),
            pltpu.VMEM((512, H), F32),
            pltpu.VMEM((8, H), F32),
        ],
        compiler_params=pltpu.CompilerParams(
            dimension_semantics=("arbitrary",), vmem_limit_bytes=56 * MIB
        ),
        name="backward",
    )(edge_count, edge_feat, grad_edges, snd, rcv, he, ds, node_feat, agg, grad_nodes, hn, dsn, gc, ct,
      rw, halo, edge_in, edge_out, node_in, node_out)

    w_all, b_all, q_all, back = pl.pallas_call(
        sum_kernel,
        out_shape=[shape((WROWS, H)), shape((8, H), F32), shape((GC, H)), shape((256, H))],
        in_specs=whole(7),
        out_specs=whole(4),
        scratch_shapes=[
            pltpu.VMEM((WROWS, H), BF),
            pltpu.VMEM((NG - 1, RA, H), BF),
            pltpu.VMEM((NR - 1, RB, H), BF),
            pltpu.VMEM((RA, H), F32),
            pltpu.VMEM((RB, H), F32),
            pltpu.VMEM((NR - 1, RA // 8, 128), F32),
            pltpu.VMEM((NG - 1, RB // 4, 128), F32),
            pltpu.VMEM((RA // 8, 128), F32),
            pltpu.VMEM((RB // 4, 128), F32),
            pltpu.VMEM((RA, H), F32),
            pltpu.VMEM((RB, H), F32),
            pltpu.VMEM((8, H), F32),
            pltpu.VMEM((8, H), F32),
            pltpu.VMEM((NG - 1, 8, H), F32),
            pltpu.VMEM((NR - 1, 8, H), F32),
            pltpu.VMEM((256, H), BF),
        ]
        + sems(8, 8, 7, 7, 7, 7, 15, 15, 15, 15, 7, 7, 15, 15, 7, 7, 7, 7, 15, 15, 7, 7, 15, 15),
        compiler_params=comm(2, 40),
        name="sums",
    )(wl, wn, wc, bias, cb, dh, q)

    outs = pl.pallas_call(
        result_kernel,
        out_shape=[
            shape((NF, H), F32), shape((NF, H), F32), shape((768, H), F32), shape((1, H), F32),
            shape((H, H), F32), shape((512, H), F32), shape((1, H), F32), shape((H, H), F32),
            shape((H, H), F32), shape((1, H), F32), shape((H, H), F32), shape((H, H), F32),
        ],
        in_specs=whole(10),
        out_specs=whole(12),
        compiler_params=pltpu.CompilerParams(vmem_limit_bytes=40 * MIB),
        name="results",
    )(w_all, b_all, q_all, back, dn, y, ct, pw, hidx, prolong)
    node_result, d_node_feat = outs[:2]
    grads = [o.reshape(H) if o.shape[0] == 1 else o for o in outs[2:]]
    return (node_result, edge_new, d_node_feat, d_edge_feat, *grads)


def solution(mesh):
    wide = P(("row", "grp"), None)
    line = P(("row", "grp"))
    in_specs = (
        (wide, wide, line, line, line, P(("row", "grp"), None, None), line, line, line)
        + (P(),) * 10
        + (wide, wide)
    )
    out_specs = (wide,) * 4 + (P(),) * 10
    return jax.shard_map(body, mesh=mesh, in_specs=in_specs, out_specs=out_specs, check_vma=False)
```

time: 385 us -> 129 us (0.34)
  Pallas kernels: 0 us -> 109 us
  blocking collectives: 97.2 us -> 0 us
  waiting for transfers between devices: 91.6 us -> 0 us
  matrix products: 74.1 us -> 0 us
  local copies, waits for them, and re-layouts: 74.1 us -> 16.4 us
  starting transfers between devices: 19.5 us -> 0 us
  between operations: 15.5 us -> 1.51 us
  other arithmetic: 9.38 us -> 0 us
    pallas_call x0 -> x6, Pallas kernels: none -> 109 us  [the longest x1 38.2 us: body(): pl.pallas_call(sum_kernel, out_shape=[shape((WROWS, H)), shape((8, H), F3...]
    dot_general x34 -> x0, matrix products: 74.1 us -> none  [the longest x15 40.5 us: contract_rows(): lax.dot_general(a, b, (((0,), (0,)), ((), ())), preferred_element_type=jn...]
    psum x1 -> x0, blocking collectives: 67.9 us -> none  [body(): all_grads = lax.psum(other_grads + coarse_grads, ('row', 'grp'))]
    gather x6 -> x0, local copies, waits for them, and re-layouts: 62.3 us -> none  [the longest x1 18.3 us: body(): sent_rows = extended[senders]]
    psum x1 -> x0, waiting for transfers between devices: 60.1 us -> none  [body(): all_grads = lax.psum(other_grads + coarse_grads, ('row', 'grp'))]
    reduce_scatter x2 -> x0, waiting for transfers between devices: 29.5 us -> none  [the longest x1 29.5 us: body(): lax.psum_scatter(partial_sum, 'grp', scatter_dimension=0, tiled=True)]
    all_gather x2 -> x0, blocking collectives: 29.3 us -> none  [the longest x1 16.4 us: body(): grad_rows = lax.all_gather(grad_c.astype(bf), 'grp', axis=0, tiled=True)]
    ppermute x8 -> x0, starting transfers between devices: 19.4 us -> none  [from_behind(): lax.ppermute(value, axis, [(source, source + steps) for source in range(i...]
  transfers between devices with their start and end apart: 11 -> 0, of which waited for: 3 -> 0; matrix products, arithmetic and copies ran while one was open for 21% -> 0% of each run, Pallas kernels for 0% -> 0%
where the time goes in v1:
time: 129 us; the launch traced here: 127 us
  Pallas kernels  109 us (84%)
  local copies, waits for them, and re-layouts  16.4 us (13%)
  between operations  1.51 us (1%)
    pallas_call x1, Pallas kernels, body(): pl.pallas_call(sum_kernel, out_shape=[shape((WROWS, H)), shape((8, H), F3...  38.2 us
    pallas_call x1, Pallas kernels, body(): pl.pallas_call(backward_kernel, grid=(blocks,), out_shape=[shape((EF, H),...  21.1 us
    pallas_call x1, Pallas kernels, body(): pl.pallas_call(edge_forward_kernel, grid=(blocks,), out_shape=[shape((EF,...  18.9 us
    pallas_call x1, Pallas kernels, body(): pl.pallas_call(halo_kernel, out_shape=[shape((NT, H)), shape((256, H)), s...  15.5 us
    unnamed x56, local copies, waits for them, and re-layouts  13.9 us
    pallas_call x1, Pallas kernels, body(): pl.pallas_call(coarse_kernel, out_shape=[shape((NF, H), F32), shape((NF,...  12.5 us
    pallas_call x1, Pallas kernels, body(): pl.pallas_call(result_kernel, out_shape=[shape((NF, H), F32), shape((NF,...  3.16 us

profile of v1, /device:TPU:1, one launch (start us, length us, event | category | flops | bytes accessed | tf_op | source)
XLA Modules:
  0.0 127.2 jit_solution(61951256270100511)
XLA Ops:
  1.3 1.2 reshape.69.ebias
  2.5 0.7 reshape.70.nbias
  3.2 0.7 reshape.72.cbias
  3.8 1.0 copy-done
  4.9 1.0 copy-done.2
  5.9 1.0 copy-done.4
  6.9 0.7 copy-done.19
  7.6 0.7 copy-done.22
  8.3 0.7 copy-done.24
  9.0 15.5 %halo.1 = (bf16[2304,256]{1,0:T(8,128)(2,1)S(1)}, bf16[256,256]{1,0:T(8,128)(2,1)S(1)}, bf16[64,256]{1,0:T(8,128)(2,1)S(1)}) custom-call(bf16[1024,256]{1,0:T(8,128)(2,1)S(1)} %copy-done, s32[8,32]{1,0:T(8,128)S(1)} %bitcast.13, s32[8,128]{1,0:T(8,128)S(1)} %bitcast.10, bf16[8,128]{1,0:T(8,128)(2,1)S(1)} %bitcast.15, bf16[1024,256]{1,0:T(8,128)(2,1)S(1)} %copy-done.4, ...), custom_call_target="tpu_custom_call" | custom-call | tf_op jit(solution)/shard_map/halo/pallas_call | solution.py:506
  24.4 1.0 copy-done.5
  26.2 18.9 %edge_forward.1 = (f32[4096,256]{1,0:T(8,128)}, bf16[4096,256]{1,0:T(8,128)(2,1)}, bf16[4096,256]{1,0:T(8,128)(2,1)}, bf16[1024,256]{1,0:T(8,128)(2,1)}) custom-call(s32[1]{0:T(128)S(6)} %copy.35.count, bf16[4096,256]{1,0:T(8,128)(2,1)} %ef.3, s32[32,128]{1,0:T(8,128)} %bitcast.19, s32[32,128]{1,0:T(8,128)} %bitcast.21, bf16[2304,256]{1,0:T(8,128)(2,1)} %copy-done.5, ...), custom_call_target="tpu_custom_call" | custom-call | tf_op jit(solution)/shard_map/edge_forward/pallas_call | solution.py:531
  45.1 1.0 copy-done.3
  46.2 12.5 %coarse.1 = (f32[1024,256]{1,0:T(8,128)S(1)}, bf16[1024,256]{1,0:T(8,128)(2,1)S(1)}, bf16[1024,256]{1,0:T(8,128)(2,1)S(1)}, bf16[512,256]{1,0:T(8,128)(2,1)S(1)}...) custom-call(bf16[1024,256]{1,0:T(8,128)(2,1)S(1)} %copy-done.1, ...), custom_call_target="tpu_custom_call" | custom-call | tf_op jit(solution)/shard_map/coarse/pallas_call | solution.py:547
  58.7 0.8 copy-done.10
  59.5 0.8 copy-done.11
  60.3 0.7 copy-done.14
  61.0 21.1 %backward.1 = (f32[4096,256]{1,0:T(8,128)}, bf16[1024,256]{1,0:T(8,128)(2,1)}, bf16[768,256]{1,0:T(8,128)(2,1)}, f32[8,256]{1,0:T(8,128)}, f32[1024,256]{1,0:T(8,128)}, /*index=5*/bf16[256,256]{1,0:T(8,128)(2,1)}) custom-call(s32[1]{0:T(128)S(6)} %copy.35.count, bf16[4096,256]{1,0:T(8,128)(2,1)} %ef.3, bf16[4096,256]{1,0:T(8,128)(2,1)} %ge.1, ...), custom_call_target="tpu_custom_call" | custom-call | tf_op jit(solution)/shard_map/backward/pallas_call | solution.py:565
  82.1 1.1 copy-done.12
  83.2 1.0 copy-done.13
  84.2 0.9 copy-done.18
  85.1 0.7 copy-done.26
  85.8 38.2 %sums.1 = (bf16[2560,256]{1,0:T(8,128)(2,1)S(1)}, f32[8,256]{1,0:T(8,128)S(1)}, bf16[512,256]{1,0:T(8,128)(2,1)S(1)}, bf16[256,256]{1,0:T(8,128)(2,1)S(1)}) custom-call(bf16[1024,256]{1,0:T(8,128)(2,1)S(1)} %copy-done.12, bf16[768,256]{1,0:T(8,128)(2,1)S(1)} %copy-done.13, bf16[768,256]{1,0:T(8,128)(2,1)S(1)} %get-tuple-element.61.wc, ...), custom_call_target="tpu_custom_call" | custom-call | tf_op jit(solution)/shard_map/sums/pallas_call | solution.py:595
  124.1 3.2 %results.1 = (f32[1024,256]{1,0:T(8,128)}, f32[1024,256]{1,0:T(8,128)}, f32[768,256]{1,0:T(8,128)}, f32[1,256]{1,0:T(1,128)}, f32[256,256]{1,0:T(8,128)}, /*inde...) custom-call(bf16[2560,256]{1,0:T(8,128)(2,1)S(1)} %get-tuple-element, ...), custom_call_target="tpu_custom_call" | custom-call | tf_op jit(solution)/shard_map/results/pallas_call | solution.py:623
  (41 shorter events, 0.7 us)
Async XLA Ops:
  3.8 1.0 copy-start
  4.9 1.0 copy-start.2
  5.9 1.0 copy-start.4
  24.4 1.0 copy-start.5
  26.1 18.9 %copy-start.1 = (bf16[1024,256]{1,0:T(8,128)(2,1)S(1)}, bf16[1024,256]{1,0:T(8,128)(2,1)}, u32[]{:S(2)}) copy-start(bf16[1024,256]{1,0:T(8,128)(2,1)} %nf.5) | copy-start | bytes 1572868
  26.1 18.9 %copy-start.7 = (bf16[512,256]{1,0:T(8,128)(2,1)S(1)}, bf16[512,256]{1,0:T(8,128)(2,1)}, u32[]{:S(2)}) copy-start(bf16[512,256]{1,0:T(8,128)(2,1)} %nin.3) | copy-start | bytes 786436
  26.1 18.9 %copy-start.8 = (bf16[256,256]{1,0:T(8,128)(2,1)S(1)}, bf16[256,256]{1,0:T(8,128)(2,1)}, u32[]{:S(2)}) copy-start(bf16[256,256]{1,0:T(8,128)(2,1)} %nout.3) | copy-start | bytes 393220
  26.1 18.9 %copy-start.9 = (bf16[256,256]{1,0:T(8,128)(2,1)S(1)}, bf16[256,256]{1,0:T(8,128)(2,1)}, u32[]{:S(2)}) copy-start(bf16[256,256]{1,0:T(8,128)(2,1)} %prol.3) | copy-start | bytes 393220
  26.1 19.0 %copy-start.16 = (bf16[256,256]{1,0:T(8,128)(2,1)S(1)}, bf16[256,256]{1,0:T(8,128)(2,1)}, u32[]{:S(2)}) copy-start(bf16[256,256]{1,0:T(8,128)(2,1)} %cin.1) | copy-start | bytes 393220
  26.1 19.0 %copy-start.17 = (bf16[256,256]{1,0:T(8,128)(2,1)S(1)}, bf16[256,256]{1,0:T(8,128)(2,1)}, u32[]{:S(2)}) copy-start(bf16[256,256]{1,0:T(8,128)(2,1)} %cout.1) | copy-start | bytes 393220
  26.1 18.9 %copy-start.20 = (s32[1024]{0:T(1024)S(1)}, s32[1024]{0:T(1024)}, u32[]{:S(2)}) copy-start(s32[1024]{0:T(1024)} %param.27) | copy-start | bytes 12292
  26.2 18.9 %copy-start.27 = (bf16[1024]{0:T(1024)(128)(2,1)S(1)}, bf16[1024]{0:T(1024)(128)(2,1)}, u32[]{:S(2)}) copy-start(bf16[1024]{0:T(1024)(128)(2,1)} %param.28) | copy-start | bytes 6148
  45.1 1.0 copy-start.3
  58.7 0.8 copy-start.10
  59.5 0.8 copy-start.11
  60.3 0.7 copy-start.14
  61.0 63.1 %copy-start.21 = (s32[1024]{0:T(1024)S(1)}, s32[1024]{0:T(1024)}, u32[]{:S(2)}) copy-start(s32[1024]{0:T(1024)} %param.27) | copy-start | bytes 12292
  61.0 63.1 %copy-start.23 = (s32[1,8,32]{2,1,0:T(8,128)S(1)}, s32[1,8,32]{2,1,0:T(8,128)}, u32[]{:S(2)}) copy-start(s32[1,8,32]{2,1,0:T(8,128)} %param.26) | copy-start | bytes 3076
  61.0 63.1 %copy-start.25 = (bf16[1024]{0:T(1024)(128)(2,1)S(1)}, bf16[1024]{0:T(1024)(128)(2,1)}, u32[]{:S(2)}) copy-start(bf16[1024]{0:T(1024)(128)(2,1)} %param.29) | copy-start | bytes 6148
  82.1 42.0 %copy-start.6 = (f32[1024,256]{1,0:T(8,128)S(1)}, f32[1024,256]{1,0:T(8,128)}, u32[]{:S(2)}) copy-start(f32[1024,256]{1,0:T(8,128)} %get-tuple-element.70.dn) | copy-start | bytes 3145732
  82.1 1.1 copy-start.12
  83.2 1.0 copy-start.13
  84.2 0.9 copy-start.18
  85.1 0.7 copy-start.26
  (4 other events, 2.7 us)

commit v2 on v1

v2 whole, which is shorter than its diff:
```python
import jax
import jax.numpy as jnp
from jax import lax
from jax.experimental import pallas as pl
from jax.experimental.pallas import tpu as pltpu
from jax.sharding import PartitionSpec as P

BF = jnp.bfloat16
F32 = jnp.float32
I32 = jnp.int32
MESH = pl.DeviceIdType.MESH
OFFSETS = ((-1, -1), (-1, 0), (-1, 1), (0, -1), (0, 1), (1, -1), (1, 0), (1, 1))
NR, NG = 16, 8
H = 256
NF = 1024
EF = 4096
NX = 1280
NT = NX + NF
GC = 512
NC = 64
BLK = 1024
SUB = 512
MIB = 1024 * 1024
LIMIT = 60


def mm(a, b):
    return lax.dot_general(a, b, (((1,), (0,)), ((), ())), preferred_element_type=F32)


def mm_nt(a, b):
    return lax.dot_general(a, b, (((1,), (1,)), ((), ())), preferred_element_type=F32)


def mm_tn(a, b):
    return lax.dot_general(a, b, (((0,), (0,)), ((), ())), preferred_element_type=F32)


def silu_parts(u):
    sg = jax.nn.sigmoid(u)
    return u * sg, sg * (1.0 + u * (1.0 - sg))


def hot_rows(idx, lo, count, weight=None):
    parts = []
    for j in range(idx.shape[0]):
        place = lax.broadcasted_iota(I32, (count, 128), 0) + lo
        value = 1.0 if weight is None else weight[j : j + 1, :]
        parts.append(jnp.where(place == idx[j : j + 1, :], value, 0.0).astype(BF))
    return jnp.concatenate(parts, axis=1)


def hot_cols(idx_t, lo, count, weight_t=None):
    parts = []
    for j in range(idx_t.shape[1]):
        place = lax.broadcasted_iota(I32, (128, count), 1) + lo
        value = 1.0 if weight_t is None else weight_t[:, j : j + 1]
        parts.append(jnp.where(place == idx_t[:, j : j + 1], value, 0.0).astype(BF))
    return jnp.concatenate(parts, axis=0)


def halo_columns(hidx):
    wide = hidx.astype(F32)
    eye = lax.broadcasted_iota(I32, (32, 32), 0) == lax.broadcasted_iota(I32, (32, 32), 1)
    return [
        jnp.sum(jnp.where(eye, wide[d : d + 1, :], 0.0), axis=1, keepdims=True) for d in range(8)
    ]


def halo_pick(hidx, lo, count):
    place = (lax.broadcasted_iota(I32, (32, count), 1) + lo).astype(F32)
    return jnp.concatenate(
        [jnp.where(place == c, 1.0, 0.0).astype(BF) for c in halo_columns(hidx)], axis=0
    )


def here():
    return lax.axis_index("row"), lax.axis_index("grp")


def shifted(r, g, dr, dg):
    return lax.rem(r + dr + NR, NR), lax.rem(g + dg + NG, NG)


def inside(r, g, dr, dg):
    rr, gg = r + dr, g + dg
    return (rr >= 0) & (rr < NR) & (gg >= 0) & (gg < NG)


def greet(r, g, steps):
    barrier = pltpu.get_barrier_semaphore()
    for dr, dg in steps:
        pl.semaphore_signal(
            barrier, inc=1, device_id=shifted(r, g, dr, dg), device_id_type=MESH
        )
    return lambda: pl.semaphore_wait(barrier, len(steps))


def over(n, fn):
    def step(k, carry):
        fn(k)
        return carry

    lax.fori_loop(1, n, step, 0)


def remote(src, dst, send, recv, place):
    return pltpu.make_async_remote_copy(
        src_ref=src, dst_ref=dst, send_sem=send, recv_sem=recv, device_id=place, device_id_type=MESH
    )


def rows(start, size):
    return pl.ds(pl.multiple_of(start * size, size), size)


GRP_STEPS = [(0, k) for k in range(1, NG)]
ROW_STEPS = [(k, 0) for k in range(1, NR)]
NEAR_STEPS = [(dr, dg) for dr, dg in OFFSETS]
HALO_PEERS = GRP_STEPS + [s for s in NEAR_STEPS if s[0] != 0]
ALL_PEERS = GRP_STEPS + ROW_STEPS + [s for s in NEAR_STEPS if s[0] != 0 and s[1] != 0]


def scatter_grp(r, g, part, land, send, recv, size):
    def copy(k):
        t = lax.rem(g + k, NG)
        return remote(part.at[rows(t, size)], land.at[k - 1], send.at[k - 1], recv.at[k - 1], (r, t))

    return copy


def fetch(pairs, sem):
    copies = [pltpu.make_async_copy(src, dst, sem.at[i]) for i, (src, dst) in enumerate(pairs)]
    for c in copies:
        c.start()

    def wait(*which):
        for i in which:
            copies[i].wait()

    return wait


def halo_kernel(hidx, ct, nf_h, pw_h, gz_h, ein_h, p_out, halo_out, s_out,
                nf, pw, gz, ein, own, land, part, sland, ls, hs, hr, ss, sr):
    r, g = here()
    ready = greet(r, g, HALO_PEERS)
    loaded = fetch([(nf_h, nf), (gz_h, gz), (pw_h, pw), (ein_h, ein)], ls)
    pick = halo_pick(hidx[...], 0, NF)
    loaded(0)
    own[...] = mm(pick, nf[...]).astype(BF)
    ready()
    halo = [
        remote(
            own.at[pl.ds(32 * d, 32)], land.at[pl.ds(32 * d, 32)], hs.at[d], hr.at[d],
            shifted(r, g, dr, dg),
        )
        for d, (dr, dg) in enumerate(OFFSETS)
    ]
    for c in halo:
        c.start()
    loaded(1, 2)
    part[...] = mm(hot_rows(ct[...], 0, GC, pw[...].astype(F32)), gz[...]).astype(BF)
    scat = scatter_grp(r, g, part, sland, ss, sr, NC)
    over(NG, lambda k: scat(k).start())
    loaded(3)
    p_out[0:NF] = mm(nf[...], ein[H : 2 * H]).astype(BF)
    p_out[NX:] = mm(nf[...], ein[2 * H :]).astype(BF)
    for c in halo:
        c.wait()
    for d, (dr, dg) in enumerate(OFFSETS):
        got = land[32 * d : 32 * d + 32]
        halo_out[32 * d : 32 * d + 32] = jnp.where(inside(r, g, -dr, -dg), got, jnp.zeros_like(got))
    p_out[NF:NX] = mm(halo_out[...], ein[H : 2 * H]).astype(BF)
    over(NG, lambda k: scat(k).wait())
    total = part[rows(g, NC)].astype(F32)
    for k in range(NG - 1):
        total += sland[k].astype(F32)
    s_out[...] = total.astype(BF)


def mask_of(count, start, size):
    place = lax.broadcasted_iota(I32, (size, 1), 0) + start
    return jnp.where(place < count, 1.0, 0.0)


def edge_forward_kernel(count, ef, snd, rcv, ptab, ein, ebias, eout, en_out, he_out, ds_out, agg_out,
                        acc):
    step = pl.program_id(0)

    @pl.when(step == 0)
    def _():
        acc[...] = jnp.zeros_like(acc)

    snd_t = jnp.transpose(snd[...])
    rcv_t = jnp.transpose(rcv[...])
    bias = ebias[...].astype(F32)
    per = SUB // 128
    for h in range(BLK // SUB):
        at = slice(h * SUB, (h + 1) * SUB)
        lanes = slice(h * per, (h + 1) * per)
        x = ef[at]
        u = mm(x, ein[0:H]) + bias
        u += mm(hot_cols(snd_t[:, lanes], 0, NX), ptab[0:NX])
        u += mm(hot_cols(rcv_t[:, lanes], 0, NF), ptab[NX:])
        s, slope = silu_parts(u)
        he = s.astype(BF)
        he_out[at] = he
        ds_out[at] = slope.astype(BF)
        m = mask_of(count[0], step * BLK + h * SUB, SUB)
        new = x.astype(F32) + m * mm(he, eout[...])
        en_out[at] = new
        acc[...] += mm(hot_rows(rcv[lanes], 0, NF), (m * new).astype(BF))

    @pl.when(step == pl.num_programs(0) - 1)
    def _():
        agg_out[...] = acc[...].astype(BF)


W_LATE, W_EARLY = 1024, 1536
WROWS = W_LATE + W_EARLY


def lanes_half(p):
    return pl.ds(pl.multiple_of(lax.rem(p, 2) * 128, 128), 128)


class Total:
    def __init__(self, r, g, wbuf, out, base, na, nb, scratch):
        self.r, self.g, self.wbuf, self.out = r, g, wbuf, out
        self.base, self.na, self.nb = base, na, nb
        self.ra, self.rb = na // NG, nb // NR
        self.pa, self.pb = self.ra // 8, self.rb // 4
        (self.a1, self.b1, self.acc_a, self.acc_b, self.a2, self.b2, self.mine_a, self.mine_b,
         self.all_a, self.all_b, *self.sems) = scratch

    @staticmethod
    def scratch(na, nb):
        ra, rb = na // NG, nb // NR
        counts = [NG - 1, NR - 1, NR - 1, NG - 1, NR - 1, NG - 1, NG - 1, NR - 1]
        return [
            pltpu.VMEM((NG - 1, ra, H), BF),
            pltpu.VMEM((NR - 1, rb, H), BF),
            pltpu.VMEM((ra, H), F32),
            pltpu.VMEM((rb, H), F32),
            pltpu.VMEM((NR - 1, ra // 8, 128), F32),
            pltpu.VMEM((NG - 1, rb // 4, 128), F32),
            pltpu.VMEM((ra // 8, 128), F32),
            pltpu.VMEM((rb // 4, 128), F32),
            pltpu.VMEM((ra, H), F32),
            pltpu.VMEM((rb, H), F32),
        ] + [pltpu.SemaphoreType.DMA((n,)) for n in counts for _ in range(2)]

    def block_a(self, t):
        return pl.ds(pl.multiple_of(self.base + t * self.ra, 16), self.ra)

    def block_b(self, t):
        return pl.ds(pl.multiple_of(self.base + self.na + t * self.rb, 16), self.rb)

    def copy(self, stage, src, dst, k, place):
        send, recv = self.sems[2 * stage], self.sems[2 * stage + 1]
        return remote(src, dst, send.at[k - 1], recv.at[k - 1], place)

    def grp(self, k):
        return lax.rem(self.g + k, NG)

    def row(self, k):
        return lax.rem(self.r + k, NR)

    def one_a(self, k):
        t = self.grp(k)
        return self.copy(0, self.wbuf.at[self.block_a(t)], self.a1.at[k - 1], k, (self.r, t))

    def one_b(self, k):
        t = self.row(k)
        return self.copy(1, self.wbuf.at[self.block_b(t)], self.b1.at[k - 1], k, (t, self.g))

    def two_a(self, k):
        t = self.row(k)
        src = self.acc_a.at[rows(t // 2, self.pa), lanes_half(t)]
        return self.copy(2, src, self.a2.at[k - 1], k, (t, self.g))

    def two_b(self, k):
        t = self.grp(k)
        src = self.acc_b.at[rows(t // 2, self.pb), lanes_half(t)]
        return self.copy(3, src, self.b2.at[k - 1], k, (self.r, t))

    def three_a(self, k):
        dst = self.all_a.at[rows(self.r // 2, self.pa), lanes_half(self.r)]
        return self.copy(4, self.mine_a, dst, k, (self.row(k), self.g))

    def three_b(self, k):
        dst = self.all_b.at[rows(self.g // 2, self.pb), lanes_half(self.g)]
        return self.copy(5, self.mine_b, dst, k, (self.r, self.grp(k)))

    def four_a(self, k):
        at = self.out.at[self.block_a(self.g)]
        return self.copy(6, at, at, k, (self.r, self.grp(k)))

    def four_b(self, k):
        at = self.out.at[self.block_b(self.r)]
        return self.copy(7, at, at, k, (self.row(k), self.g))

    def start_one(self):
        over(NR, lambda k: self.one_b(k).start())
        over(NG, lambda k: self.one_a(k).start())

    def start_two(self):
        over(NR, lambda k: self.one_b(k).wait())
        total = self.wbuf[self.block_b(self.r)].astype(F32)
        for k in range(NR - 1):
            total += self.b1[k].astype(F32)
        self.acc_b[...] = total
        over(NG, lambda k: self.two_b(k).start())
        over(NG, lambda k: self.one_a(k).wait())
        total = self.wbuf[self.block_a(self.g)].astype(F32)
        for k in range(NG - 1):
            total += self.a1[k].astype(F32)
        self.acc_a[...] = total
        over(NR, lambda k: self.two_a(k).start())

    def start_three(self):
        over(NG, lambda k: self.two_b(k).wait())
        at = rows(self.g // 2, self.pb), lanes_half(self.g)
        total = self.acc_b[at]
        for k in range(NG - 1):
            total += self.b2[k]
        self.mine_b[...] = total
        self.all_b[at] = total
        over(NG, lambda k: self.three_b(k).start())
        over(NR, lambda k: self.two_a(k).wait())
        at = rows(self.r // 2, self.pa), lanes_half(self.r)
        total = self.acc_a[at]
        for k in range(NR - 1):
            total += self.a2[k]
        self.mine_a[...] = total
        self.all_a[at] = total
        over(NR, lambda k: self.three_a(k).start())

    def start_four(self):
        over(NG, lambda k: self.three_b(k).wait())
        self.out[self.block_b(self.r)] = self.all_b[...].astype(BF)
        over(NR, lambda k: self.four_b(k).start())
        over(NR, lambda k: self.three_a(k).wait())
        self.out[self.block_a(self.g)] = self.all_a[...].astype(BF)
        over(NG, lambda k: self.four_a(k).start())

    def finish(self):
        over(NR, lambda k: self.four_b(k).wait())
        over(NG, lambda k: self.four_a(k).wait())


LATE = (512, 512)
EARLY = (1024, 512)


def rear_kernel(count, nf_h, agg_h, nin_h, nbias_h, nout_h, ct, rw_h, s_h, cin_h, cbias_h, cout_h,
                prol_h, gz_h, ef_h, ge_h, snd, rcv, he_h, ds_h, halo_h, ein_h, eout_h,
                w_out, b_out, q_out, h_out, y_out, dn_out, def_out,
                nf, agg, nin, nbias, nout, rw, s_in, cin, cbias, cout, prol, gz, ef, ge, he, ds, halo,
                ein, eout, ls,
                y, hn, dsn, part, cland, gc_own, gc, q_own, gagg, gyn, ssum, wacc, wbuf, defb, dh, hland,
                bias0, bias1, bl1, bl2,
                css, csr, cgs, cgr, qs, qr, hs, hr, c1s, c1r, c2s, c2r, outs, *sums):
    r, g = here()
    ready = greet(r, g, ALL_PEERS)
    half_way = len(sums) // 2
    early = Total(r, g, wbuf, w_out, W_LATE, *EARLY, sums[:half_way])
    late = Total(r, g, wbuf, w_out, 0, *LATE, sums[half_way:])
    loaded = fetch(
        [(nf_h, nf), (agg_h, agg), (nin_h, nin), (nbias_h, nbias), (nout_h, nout), (rw_h, rw),
         (s_h, s_in), (cin_h, cin), (cbias_h, cbias), (cout_h, cout), (prol_h, prol), (gz_h, gz),
         (eout_h, eout), (ein_h, ein), (halo_h, halo), (ge_h, ge), (ds_h, ds), (ef_h, ef), (he_h, he)],
        ls,
    )

    def grp(k):
        return (r, lax.rem(g + k, NG))

    loaded(0, 1, 2, 3)
    un = mm(nf[...], nin[0:H]) + mm(agg[...], nin[H:]) + nbias[...].astype(F32)
    s, slope = silu_parts(un)
    hn[...] = s.astype(BF)
    dsn[...] = slope.astype(BF)
    loaded(4, 5)
    fresh = nf[...].astype(F32) + mm(hn[...], nout[...])
    y[...] = fresh
    part[...] = mm(hot_rows(ct[...], 0, GC, rw[...].astype(F32)), fresh.astype(BF)).astype(BF)
    ready()
    scat = scatter_grp(r, g, part, cland, css, csr, NC)
    over(NG, lambda k: scat(k).start())
    keep_y = pltpu.make_async_copy(y, y_out, outs.at[0])
    keep_y.start()

    loaded(6, 7, 8, 9, 10)
    sb = s_in[...]
    gcn = mm_nt(sb, prol[...])
    gcnb = gcn.astype(BF)
    gh = mm_nt(gcnb, cout[...])
    over(NG, lambda k: scat(k).wait())
    c = part[rows(g, NC)].astype(F32)
    for k in range(NG - 1):
        c += cland[k].astype(F32)
    cb = c.astype(BF)
    uc = mm(cb, cin[...]) + cbias[...].astype(F32)
    s, slope = silu_parts(uc)
    hc = s.astype(BF)
    guc = gh * slope
    gucb = guc.astype(BF)
    gco = (gcn + mm_nt(gucb, cin[...])).astype(BF)
    gc_own[...] = gco
    gc[rows(g, NC)] = gco

    def give_gc(k):
        return remote(gc_own, gc.at[rows(g, NC)], cgs.at[k - 1], cgr.at[k - 1], grp(k))

    over(NG, lambda k: give_gc(k).start())
    q = (c + mm(hc, cout[...])).astype(BF)
    q_own[...] = q
    q_out[rows(g, NC)] = q

    def give_q(k):
        return remote(q_own, q_out.at[rows(g, NC)], qs.at[k - 1], qr.at[k - 1], grp(k))

    over(NG, lambda k: give_q(k).start())
    wbuf[1792:2048] = mm_tn(cb, gucb).astype(BF)
    wbuf[2048:2304] = mm_tn(hc, gcnb).astype(BF)
    wbuf[2304:2560] = mm_tn(q, sb).astype(BF)
    bias0[...] = jnp.zeros_like(bias0)
    bias0[2:3] = jnp.sum(guc, axis=0, keepdims=True)
    ssum[...] = jnp.zeros_like(ssum)
    wacc[...] = jnp.zeros_like(wacc)
    table = hot_cols(jnp.transpose(ct[...]), 0, GC, jnp.transpose(rw[...].astype(F32)))
    loaded(11)
    over(NG, lambda k: give_gc(k).wait())

    gy = gz[...].astype(F32) + mm(table, gc[...])
    gyb = gy.astype(BF)
    gun = mm_nt(gyb, nout[...]) * dsn[...].astype(F32)
    gunb = gun.astype(BF)
    gagg[...] = mm_nt(gunb, nin[H:]).astype(BF)
    gyn[...] = gy + mm_nt(gunb, nin[0:H])
    wbuf[1024:1280] = mm_tn(nf[...], gunb).astype(BF)
    wbuf[1280:1536] = mm_tn(agg[...], gunb).astype(BF)
    wbuf[1536:1792] = mm_tn(hn[...], gyb).astype(BF)
    bias0[1:2] = jnp.sum(gun, axis=0, keepdims=True)
    early.start_one()

    loaded(12, 13, 14, 15, 16, 17, 18)
    per = SUB // 128

    def keep(step):
        at = pl.ds(pl.multiple_of(step * BLK, BLK), BLK)
        return pltpu.make_async_copy(defb.at[at], def_out.at[at], outs.at[2 + step])

    def edges(step, carry):
        @pl.when(step == 1)
        def _():
            early.start_two()

        @pl.when(step == 2)
        def _():
            early.start_three()

        @pl.when(step == 3)
        def _():
            early.start_four()

        at8 = pl.ds(pl.multiple_of(step * (BLK // 128), BLK // 128), BLK // 128)
        snd8, rcv8 = snd[at8], rcv[at8]
        rcv_t = jnp.transpose(rcv8)
        for h in range(BLK // SUB):
            at = pl.ds(pl.multiple_of(step * BLK + h * SUB, SUB), SUB)
            lanes = slice(h * per, (h + 1) * per)
            m = mask_of(count[0], step * BLK + h * SUB, SUB)
            gen = ge[at].astype(F32) + m * mm(hot_cols(rcv_t[:, lanes], 0, NF), gagg[...])
            gm = (m * gen).astype(BF)
            gue = mm_nt(gm, eout[...]) * ds[at].astype(F32)
            gueb = gue.astype(BF)
            defb[at] = (gen + mm_nt(gueb, ein[0:H])).astype(BF)
            wacc[0:H] += mm_tn(ef[at], gueb)
            wacc[H:] += mm_tn(he[at], gm)
            bias0[0:1] += jnp.sum(gue, axis=0, keepdims=True)
            ssum[0:NX] += mm(hot_rows(snd8[lanes], 0, NX), gueb)
            ssum[NX:] += mm(hot_rows(rcv8[lanes], 0, NF), gueb)
        keep(step).start()
        return carry

    lax.fori_loop(0, EF // BLK, edges, 0)
    sums_b = ssum[...].astype(BF)
    dh[...] = mm_nt(sums_b[NF:NX], ein[H : 2 * H]).astype(BF)
    back = [
        remote(
            dh.at[pl.ds(32 * d, 32)], hland.at[pl.ds(32 * d, 32)], hs.at[d], hr.at[d],
            shifted(r, g, -dr, -dg),
        )
        for d, (dr, dg) in enumerate(OFFSETS)
    ]
    for b in back:
        b.start()

    def one_bias(k):
        return remote(bias0, bl1.at[k - 1], c1s.at[k - 1], c1r.at[k - 1], grp(k))

    def two_bias(k):
        return remote(bias1, bl2.at[k - 1], c2s.at[k - 1], c2r.at[k - 1], (lax.rem(r + k, NR), g))

    over(NG, lambda k: one_bias(k).start())
    wbuf[0:H] = wacc[0:H].astype(BF)
    wbuf[H : 2 * H] = (mm_tn(nf[...], sums_b[0:NF]) + mm_tn(halo[...], sums_b[NF:NX])).astype(BF)
    wbuf[2 * H : 3 * H] = mm_tn(nf[...], sums_b[NX:]).astype(BF)
    wbuf[3 * H : 4 * H] = wacc[H:].astype(BF)
    late.start_one()
    gyn[...] += mm_nt(sums_b[0:NF], ein[H : 2 * H]) + mm_nt(sums_b[NX:], ein[2 * H :])
    keep_dn = pltpu.make_async_copy(gyn, dn_out, outs.at[1])
    keep_dn.start()
    over(NG, lambda k: one_bias(k).wait())
    total = bias0[...]
    for k in range(NG - 1):
        total += bl1[k]
    bias1[...] = total
    over(NR, lambda k: two_bias(k).start())
    early.finish()
    over(NG, lambda k: give_q(k).wait())
    late.start_two()
    for b in back:
        b.wait()
    for d, (dr, dg) in enumerate(OFFSETS):
        got = hland[32 * d : 32 * d + 32]
        h_out[32 * d : 32 * d + 32] = jnp.where(inside(r, g, dr, dg), got, jnp.zeros_like(got))
    late.start_three()
    over(NR, lambda k: two_bias(k).wait())
    total = bias1[...]
    for k in range(NR - 1):
        total += bl2[k]
    b_out[...] = total
    keep_y.wait()
    keep_dn.wait()
    for step in range(EF // BLK):
        keep(step).wait()
    late.start_four()
    late.finish()


PARTS = 4


def result_kernel(b, q, back, dn, y, ct, pw, hidx, prol, de,
                  w_ein, w_eout, w_nin, w_nout, w_cin, w_cout, w_pr,
                  nr_out, dnf_out, def_out, o_eb, o_nb, o_cb,
                  o_ein, o_eout, o_nin, o_nout, o_cin, o_cout, o_pr, qp, pwf):
    step = pl.program_id(0)
    size = NF // PARTS

    @pl.when(step == 0)
    def _():
        qp[...] = mm(q[...], prol[...]).astype(BF)
        pwf[...] = pw[...].astype(F32)
        o_eb[...] = b[0:1]
        o_nb[...] = b[1:2]
        o_cb[...] = b[2:3]

    at = pl.ds(step * (size // 128), size // 128)
    table = hot_rows(ct[at], 0, GC, pwf[at])
    nr_out[...] = y[...] + mm_tn(table, qp[...])
    dnf_out[...] = dn[...] + mm_tn(halo_pick(hidx[...], step * size, size), back[...])
    def_out[...] = de[...].astype(F32)
    for dst, src in ((o_ein, w_ein), (o_eout, w_eout), (o_nin, w_nin), (o_nout, w_nout),
                     (o_cin, w_cin), (o_cout, w_cout), (o_pr, w_pr)):
        dst[...] = src[...].astype(F32)


def body(node_feat, edge_feat, senders, receivers, edge_count, halo_index, coarse_target,
         restrict_weight, prolong_weight, edge_in, edge_bias, edge_out, node_in, node_bias, node_out,
         coarse_in, coarse_bias, coarse_out, prolong, grad_nodes, grad_edges):
    snd = senders.reshape(EF // 128, 128)
    rcv = receivers.reshape(EF // 128, 128)
    ct = coarse_target.reshape(NF // 128, 128)
    rw = restrict_weight.reshape(NF // 128, 128)
    pw = prolong_weight.reshape(NF // 128, 128)
    hidx = halo_index.reshape(8, 32)
    ebias, nbias, cbias = (v.reshape(1, H) for v in (edge_bias, node_bias, coarse_bias))

    def shape(dims, dtype=BF):
        return jax.ShapeDtypeStruct(dims, dtype)

    def sems(*sizes):
        return [pltpu.SemaphoreType.DMA((n,)) for n in sizes]

    def whole(n):
        return [pl.BlockSpec(memory_space=pltpu.VMEM)] * n

    def far(n):
        return [pl.BlockSpec(memory_space=pl.ANY)] * n

    def vmem(*dims, dtype=BF):
        return pltpu.VMEM(dims, dtype)

    smem = pl.BlockSpec(memory_space=pltpu.SMEM)

    def comm(ident, limit):
        return pltpu.CompilerParams(
            collective_id=ident, has_side_effects=True, vmem_limit_bytes=limit * MIB
        )

    ptab, halo, s_own = pl.pallas_call(
        halo_kernel,
        out_shape=[shape((NT, H)), shape((256, H)), shape((NC, H))],
        in_specs=whole(2) + far(4),
        out_specs=whole(3),
        scratch_shapes=[
            vmem(NF, H), vmem(8, 128), vmem(NF, H), vmem(768, H),
            vmem(256, H), vmem(256, H), vmem(GC, H), vmem(NG - 1, NC, H),
        ]
        + sems(4, 8, 8, NG - 1, NG - 1),
        compiler_params=comm(0, LIMIT),
        name="halo",
    )(hidx, ct, node_feat, pw, grad_nodes, edge_in)

    blocks = EF // BLK

    def by_edge(width=H):
        return pl.BlockSpec((BLK, width), lambda i: (i, 0))

    def fixed(dims):
        return pl.BlockSpec(dims, lambda i: (0, 0))

    idx_spec = pl.BlockSpec((BLK // 128, 128), lambda i: (i, 0))
    edge_new, he, ds, agg = pl.pallas_call(
        edge_forward_kernel,
        grid=(blocks,),
        out_shape=[shape((EF, H), F32), shape((EF, H)), shape((EF, H)), shape((NF, H))],
        in_specs=[
            smem, by_edge(), idx_spec, idx_spec, fixed((NT, H)), fixed((768, H)), fixed((1, H)),
            fixed((H, H)),
        ],
        out_specs=[by_edge(), by_edge(), by_edge(), fixed((NF, H))],
        scratch_shapes=[pltpu.VMEM((NF, H), F32)],
        compiler_params=pltpu.CompilerParams(
            dimension_semantics=("arbitrary",), vmem_limit_bytes=LIMIT * MIB
        ),
        name="edge_forward",
    )(edge_count, edge_feat, snd, rcv, ptab, edge_in, ebias, edge_out)

    w_all, b_all, q_all, back, y, dn, de = pl.pallas_call(
        rear_kernel,
        out_shape=[
            shape((WROWS, H)), shape((8, H), F32), shape((GC, H)), shape((256, H)),
            shape((NF, H), F32), shape((NF, H), F32), shape((EF, H)),
        ],
        in_specs=[smem] + far(5) + whole(1) + far(9) + whole(2) + far(5),
        out_specs=whole(4) + far(3),
        scratch_shapes=[
            vmem(NF, H), vmem(NF, H), vmem(512, H), vmem(1, H), vmem(H, H), vmem(8, 128), vmem(NC, H),
            vmem(H, H), vmem(1, H), vmem(H, H), vmem(H, H), vmem(NF, H), vmem(EF, H), vmem(EF, H),
            vmem(EF, H), vmem(EF, H), vmem(256, H), vmem(768, H), vmem(H, H),
        ]
        + sems(19)
        + [
            vmem(NF, H, dtype=F32), vmem(NF, H), vmem(NF, H), vmem(GC, H), vmem(NG - 1, NC, H),
            vmem(NC, H), vmem(GC, H), vmem(NC, H), vmem(NF, H), vmem(NF, H, dtype=F32),
            vmem(NT, H, dtype=F32), vmem(512, H, dtype=F32), vmem(WROWS, H), vmem(EF, H),
            vmem(256, H), vmem(256, H), vmem(8, H, dtype=F32), vmem(8, H, dtype=F32),
            vmem(NG - 1, 8, H, dtype=F32), vmem(NR - 1, 8, H, dtype=F32),
        ]
        + sems(7, 7, 7, 7, 7, 7, 8, 8, 7, 7, 15, 15, 2 + blocks)
        + Total.scratch(*EARLY)
        + Total.scratch(*LATE),
        compiler_params=comm(1, LIMIT),
        name="rear",
    )(edge_count, node_feat, agg, node_in, nbias, node_out, ct, rw, s_own, coarse_in, cbias,
      coarse_out, prolong, grad_nodes, edge_feat, grad_edges, snd, rcv, he, ds, halo, edge_in, edge_out)

    def piece(size, start):
        return pl.BlockSpec((size // PARTS, H), lambda i: (start * PARTS // size + i, 0))

    sizes = (768, 256, 512, 256, 256, 256, 256)
    starts = (0, 768, 1024, 1536, 1792, 2048, 2304)
    (node_result, d_node_feat, d_edge_feat, g_eb, g_nb, g_cb, g_ein, g_eout, g_nin, g_nout, g_cin,
     g_cout, g_pr) = pl.pallas_call(
        result_kernel,
        grid=(PARTS,),
        out_shape=[shape((NF, H), F32), shape((NF, H), F32), shape((EF, H), F32)]
        + [shape((1, H), F32)] * 3
        + [shape((n, H), F32) for n in sizes],
        in_specs=[
            fixed((8, H)), fixed((GC, H)), fixed((256, H)), piece(NF, 0), piece(NF, 0), fixed((8, 128)),
            fixed((8, 128)), fixed((8, 32)), fixed((H, H)), piece(EF, 0),
        ]
        + [piece(n, at) for n, at in zip(sizes, starts)],
        out_specs=[piece(NF, 0), piece(NF, 0), piece(EF, 0)]
        + [fixed((1, H))] * 3
        + [piece(n, 0) for n in sizes],
        scratch_shapes=[vmem(GC, H), vmem(8, 128, dtype=F32)],
        compiler_params=pltpu.CompilerParams(
            dimension_semantics=("arbitrary",), vmem_limit_bytes=LIMIT * MIB
        ),
        name="results",
    )(b_all, q_all, back, dn, y, ct, pw, hidx, prolong, de, *[w_all] * 7)
    return (node_result, edge_new, d_node_feat, d_edge_feat, g_ein, g_eb.reshape(H), g_eout, g_nin,
            g_nb.reshape(H), g_nout, g_cin, g_cb.reshape(H), g_cout, g_pr)


def solution(mesh):
    wide = P(("row", "grp"), None)
    line = P(("row", "grp"))
    in_specs = (
        (wide, wide, line, line, line, P(("row", "grp"), None, None), line, line, line)
        + (P(),) * 10
        + (wide, wide)
    )
    out_specs = (wide,) * 4 + (P(),) * 10
    return jax.shard_map(body, mesh=mesh, in_specs=in_specs, out_specs=out_specs, check_vma=False)
```

time: 129 us -> 114 us (0.88); the launches traced: 127 us -> 114 us
  local copies, waits for them, and re-layouts: 16.4 us -> 3.66 us
    unnamed x56 -> x0, local copies, waits for them, and re-layouts: 13.9 us -> none
    pallas_call x4 -> x2, Pallas kernels: 75 us -> 72.9 us  [the longest x1 65.8 us: body(): pl.pallas_call(rear_kernel, out_shape=[shape((WROWS, H)), shape((8, H), F...]
    pallas_call x1, Pallas kernels: 15.5 us -> 17.3 us  [body(): pl.pallas_call(halo_kernel, out_shape=[shape((NT, H)), shape((256, H)), s...]
where the time goes in v2:
time: 114 us
  Pallas kernels  109 us (96%)
  local copies, waits for them, and re-layouts  3.66 us (3%)
  between operations  1.31 us (1%)
    pallas_call x1, Pallas kernels, body(): pl.pallas_call(rear_kernel, out_shape=[shape((WROWS, H)), shape((8, H), F...  65.8 us
    pallas_call x1, Pallas kernels, body(): pl.pallas_call(edge_forward_kernel, grid=(blocks,), out_shape=[shape((EF,...  18.8 us
    pallas_call x1, Pallas kernels, body(): pl.pallas_call(halo_kernel, out_shape=[shape((NT, H)), shape((256, H)), s...  17.3 us
    pallas_call x1, Pallas kernels, body(): pl.pallas_call(result_kernel, grid=(PARTS,), out_shape=[shape((NF, H), F3...  7.15 us
    reshape x3, local copies, waits for them, and re-layouts, body(): v.reshape(1, H)  3.66 us

profile of v2, /device:TPU:1, one launch (start us, length us, event | category | flops | bytes accessed | tf_op | source)
XLA Modules:
  0.0 114.0 jit_solution(12041576896550529120)
XLA Ops:
  1.3 1.2 %reshape.69.ebias = bf16[1,256]{1,0:T(2,128)(2,1)} reshape(bf16[256]{0:T(256)(128)(2,1)} %param.31) | data formatting | bytes 1024 | tf_op jit(solution)/shard_map/reshape | solution.py:582
  2.5 1.2 %reshape.70.nbias_h = bf16[1,256]{1,0:T(2,128)(2,1)} reshape(bf16[256]{0:T(256)(128)(2,1)} %param.34) | data formatting | bytes 1024 | tf_op jit(solution)/shard_map/reshape | solution.py:582
  3.7 1.2 %reshape.72.cbias_h = bf16[1,256]{1,0:T(2,128)(2,1)} reshape(bf16[256]{0:T(256)(128)(2,1)} %param.37) | data formatting | bytes 1024 | tf_op jit(solution)/shard_map/reshape | solution.py:582
  5.0 17.3 %halo.1 = (bf16[2304,256]{1,0:T(8,128)(2,1)}, bf16[256,256]{1,0:T(8,128)(2,1)}, bf16[64,256]{1,0:T(8,128)(2,1)}) custom-call(s32[8,32]{1,0:T(8,128)} %bitcast.16, s32[8,128]{1,0:T(8,128)} %bitcast.13, bf16[1024,256]{1,0:T(8,128)(2,1)} %nf_h.3, bf16[8,128]{1,0:T(8,128)(2,1)} %bitcast.18, bf16[1024,256]{1,0:T(8,128)(2,1)} %gz_h.3, bf16[768,256]{1,0:T(8,128)(2,1)} %ein_h.3), custom_call_target="tpu_custom_call" | custom-call | tf_op jit(solution)/shard_map/halo/pallas_call | solution.py:606
  22.2 18.8 %edge_forward.1 = (f32[4096,256]{1,0:T(8,128)}, bf16[4096,256]{1,0:T(8,128)(2,1)}, bf16[4096,256]{1,0:T(8,128)(2,1)}, bf16[1024,256]{1,0:T(8,128)(2,1)}) custom-call(s32[1]{0:T(128)S(6)} %copy.35.count, bf16[4096,256]{1,0:T(8,128)(2,1)} %ef_h.1, s32[32,128]{1,0:T(8,128)} %bitcast.9, s32[32,128]{1,0:T(8,128)} %bitcast.11, ...), custom_call_target="tpu_custom_call" | custom-call | tf_op jit(solution)/shard_map/edge_forward/pallas_call | solution.py:629
  41.0 65.8 %rear.1 = (bf16[2560,256]{1,0:T(8,128)(2,1)}, f32[8,256]{1,0:T(8,128)}, bf16[512,256]{1,0:T(8,128)(2,1)}, bf16[256,256]{1,0:T(8,128)(2,1)}, f32[1024,256]{1,0:T(...) custom-call(s32[1]{0:T(128)S(6)} %copy.35.count, bf16[1024,256]{1,0:T(8,128)(2,1)} %nf_h.3, ...), custom_call_target="tpu_custom_call" | custom-call | tf_op jit(solution)/shard_map/rear/pallas_call | solution.py:645
  106.8 7.1 %results.1 = (f32[1024,256]{1,0:T(8,128)}, f32[1024,256]{1,0:T(8,128)}, f32[4096,256]{1,0:T(8,128)}, f32[1,256]{1,0:T(1,128)}, f32[1,256]{1,0:T(1,128)}, /*index...) custom-call(f32[8,256]{1,0:T(8,128)} %get-tuple-element.47.b, ...), custom_call_target="tpu_custom_call" | custom-call | tf_op jit(solution)/shard_map/results/pallas_call | solution.py:680

commit v3 on v2

v3 whole, which is shorter than its diff:
```python
import jax
import jax.numpy as jnp
from jax import lax
from jax.experimental import pallas as pl
from jax.experimental.pallas import tpu as pltpu
from jax.sharding import PartitionSpec as P

BF = jnp.bfloat16
F32 = jnp.float32
I32 = jnp.int32
MESH = pl.DeviceIdType.MESH
OFFSETS = ((-1, -1), (-1, 0), (-1, 1), (0, -1), (0, 1), (1, -1), (1, 0), (1, 1))
NR, NG = 16, 8
H = 256
NF = 1024
EF = 4096
NX = 1280
NT = NX + NF
GC = 512
NC = 64
BLK = 1024
SUB = 512
MIB = 1024 * 1024
LIMIT = 60


def mm(a, b):
    return lax.dot_general(a, b, (((1,), (0,)), ((), ())), preferred_element_type=F32)


def mm_nt(a, b):
    return lax.dot_general(a, b, (((1,), (1,)), ((), ())), preferred_element_type=F32)


def mm_tn(a, b):
    return lax.dot_general(a, b, (((0,), (0,)), ((), ())), preferred_element_type=F32)


def silu_parts(u):
    sg = jax.nn.sigmoid(u)
    return u * sg, sg * (1.0 + u * (1.0 - sg))


def hot_rows(idx, lo, count, weight=None):
    parts = []
    for j in range(idx.shape[0]):
        place = lax.broadcasted_iota(I32, (count, 128), 0) + lo
        value = 1.0 if weight is None else weight[j : j + 1, :]
        parts.append(jnp.where(place == idx[j : j + 1, :], value, 0.0).astype(BF))
    return jnp.concatenate(parts, axis=1)


def hot_cols(idx_t, lo, count, weight_t=None):
    parts = []
    for j in range(idx_t.shape[1]):
        place = lax.broadcasted_iota(I32, (128, count), 1) + lo
        value = 1.0 if weight_t is None else weight_t[:, j : j + 1]
        parts.append(jnp.where(place == idx_t[:, j : j + 1], value, 0.0).astype(BF))
    return jnp.concatenate(parts, axis=0)


def halo_columns(hidx):
    wide = hidx.astype(F32)
    eye = lax.broadcasted_iota(I32, (32, 32), 0) == lax.broadcasted_iota(I32, (32, 32), 1)
    return [
        jnp.sum(jnp.where(eye, wide[d : d + 1, :], 0.0), axis=1, keepdims=True) for d in range(8)
    ]


def halo_pick(hidx, lo, count):
    place = (lax.broadcasted_iota(I32, (32, count), 1) + lo).astype(F32)
    return jnp.concatenate(
        [jnp.where(place == c, 1.0, 0.0).astype(BF) for c in halo_columns(hidx)], axis=0
    )


def here():
    return lax.axis_index("row"), lax.axis_index("grp")


def shifted(r, g, dr, dg):
    return lax.rem(r + dr + NR, NR), lax.rem(g + dg + NG, NG)


def inside(r, g, dr, dg):
    rr, gg = r + dr, g + dg
    return (rr >= 0) & (rr < NR) & (gg >= 0) & (gg < NG)


def greet(r, g, steps):
    barrier = pltpu.get_barrier_semaphore()
    for dr, dg in steps:
        pl.semaphore_signal(
            barrier, inc=1, device_id=shifted(r, g, dr, dg), device_id_type=MESH
        )
    return lambda: pl.semaphore_wait(barrier, len(steps))


def over(n, fn):
    def step(k, carry):
        fn(k)
        return carry

    lax.fori_loop(1, n, step, 0)


def remote(src, dst, send, recv, place):
    return pltpu.make_async_remote_copy(
        src_ref=src, dst_ref=dst, send_sem=send, recv_sem=recv, device_id=place, device_id_type=MESH
    )


def rows(start, size):
    return pl.ds(pl.multiple_of(start * size, size), size)


GRP_STEPS = [(0, k) for k in range(1, NG)]
ROW_STEPS = [(k, 0) for k in range(1, NR)]
NEAR_STEPS = [(dr, dg) for dr, dg in OFFSETS]
HALO_PEERS = GRP_STEPS + [s for s in NEAR_STEPS if s[0] != 0]
ALL_PEERS = GRP_STEPS + ROW_STEPS + [s for s in NEAR_STEPS if s[0] != 0 and s[1] != 0]


def scatter_grp(r, g, part, land, send, recv, size):
    def copy(k):
        t = lax.rem(g + k, NG)
        return remote(part.at[rows(t, size)], land.at[k - 1], send.at[k - 1], recv.at[k - 1], (r, t))

    return copy


W_LATE, W_EARLY = 1024, 1536
WROWS = W_LATE + W_EARLY


def lanes_half(p):
    return pl.ds(pl.multiple_of(lax.rem(p, 2) * 128, 128), 128)


class Total:
    def __init__(self, r, g, wbuf, out, base, na, nb, scratch):
        self.r, self.g, self.wbuf, self.out = r, g, wbuf, out
        self.base, self.na, self.nb = base, na, nb
        self.ra, self.rb = na // NG, nb // NR
        self.pa, self.pb = self.ra // 8, self.rb // 4
        (self.a1, self.b1, self.acc_a, self.acc_b, self.a2, self.b2, self.mine_a, self.mine_b,
         self.all_a, self.all_b, *self.sems) = scratch

    @staticmethod
    def scratch(na, nb):
        ra, rb = na // NG, nb // NR
        counts = [NG - 1, NR - 1, NR - 1, NG - 1, NR - 1, NG - 1, NG - 1, NR - 1]
        return [
            pltpu.VMEM((NG - 1, ra, H), BF),
            pltpu.VMEM((NR - 1, rb, H), BF),
            pltpu.VMEM((ra, H), F32),
            pltpu.VMEM((rb, H), F32),
            pltpu.VMEM((NR - 1, ra // 8, 128), F32),
            pltpu.VMEM((NG - 1, rb // 4, 128), F32),
            pltpu.VMEM((ra // 8, 128), F32),
            pltpu.VMEM((rb // 4, 128), F32),
            pltpu.VMEM((ra, H), F32),
            pltpu.VMEM((rb, H), F32),
        ] + [pltpu.SemaphoreType.DMA((n,)) for n in counts for _ in range(2)]

    def block_a(self, t):
        return pl.ds(pl.multiple_of(self.base + t * self.ra, 16), self.ra)

    def block_b(self, t):
        return pl.ds(pl.multiple_of(self.base + self.na + t * self.rb, 16), self.rb)

    def copy(self, stage, src, dst, k, place):
        send, recv = self.sems[2 * stage], self.sems[2 * stage + 1]
        return remote(src, dst, send.at[k - 1], recv.at[k - 1], place)

    def grp(self, k):
        return lax.rem(self.g + k, NG)

    def row(self, k):
        return lax.rem(self.r + k, NR)

    def one_a(self, k):
        t = self.grp(k)
        return self.copy(0, self.wbuf.at[self.block_a(t)], self.a1.at[k - 1], k, (self.r, t))

    def one_b(self, k):
        t = self.row(k)
        return self.copy(1, self.wbuf.at[self.block_b(t)], self.b1.at[k - 1], k, (t, self.g))

    def two_a(self, k):
        t = self.row(k)
        src = self.acc_a.at[rows(t // 2, self.pa), lanes_half(t)]
        return self.copy(2, src, self.a2.at[k - 1], k, (t, self.g))

    def two_b(self, k):
        t = self.grp(k)
        src = self.acc_b.at[rows(t // 2, self.pb), lanes_half(t)]
        return self.copy(3, src, self.b2.at[k - 1], k, (self.r, t))

    def three_a(self, k):
        dst = self.all_a.at[rows(self.r // 2, self.pa), lanes_half(self.r)]
        return self.copy(4, self.mine_a, dst, k, (self.row(k), self.g))

    def three_b(self, k):
        dst = self.all_b.at[rows(self.g // 2, self.pb), lanes_half(self.g)]
        return self.copy(5, self.mine_b, dst, k, (self.r, self.grp(k)))

    def four_a(self, k):
        at = self.out.at[self.block_a(self.g)]
        return self.copy(6, at, at, k, (self.r, self.grp(k)))

    def four_b(self, k):
        at = self.out.at[self.block_b(self.r)]
        return self.copy(7, at, at, k, (self.row(k), self.g))

    def start_one(self):
        over(NR, lambda k: self.one_b(k).start())
        over(NG, lambda k: self.one_a(k).start())

    def start_two(self):
        over(NR, lambda k: self.one_b(k).wait())
        total = self.wbuf[self.block_b(self.r)].astype(F32)
        for k in range(NR - 1):
            total += self.b1[k].astype(F32)
        self.acc_b[...] = total
        over(NG, lambda k: self.two_b(k).start())
        over(NG, lambda k: self.one_a(k).wait())
        total = self.wbuf[self.block_a(self.g)].astype(F32)
        for k in range(NG - 1):
            total += self.a1[k].astype(F32)
        self.acc_a[...] = total
        over(NR, lambda k: self.two_a(k).start())

    def start_three(self):
        over(NG, lambda k: self.two_b(k).wait())
        at = rows(self.g // 2, self.pb), lanes_half(self.g)
        total = self.acc_b[at]
        for k in range(NG - 1):
            total += self.b2[k]
        self.mine_b[...] = total
        self.all_b[at] = total
        over(NG, lambda k: self.three_b(k).start())
        over(NR, lambda k: self.two_a(k).wait())
        at = rows(self.r // 2, self.pa), lanes_half(self.r)
        total = self.acc_a[at]
        for k in range(NR - 1):
            total += self.a2[k]
        self.mine_a[...] = total
        self.all_a[at] = total
        over(NR, lambda k: self.three_a(k).start())

    def start_four(self):
        over(NG, lambda k: self.three_b(k).wait())
        self.out[self.block_b(self.r)] = self.all_b[...].astype(BF)
        over(NR, lambda k: self.four_b(k).start())
        over(NR, lambda k: self.three_a(k).wait())
        self.out[self.block_a(self.g)] = self.all_a[...].astype(BF)
        over(NG, lambda k: self.four_a(k).start())

    def finish(self):
        over(NR, lambda k: self.four_b(k).wait())
        over(NG, lambda k: self.four_a(k).wait())


LATE = (512, 512)
EARLY = (1024, 512)


def mask_of(count, start, size):
    place = lax.broadcasted_iota(I32, (size, 1), 0) + start
    return jnp.where(place < count, 1.0, 0.0)


def fetch(pairs, sem):
    copies = [pltpu.make_async_copy(src, dst, sem.at[i]) for i, (src, dst) in enumerate(pairs)]
    for c in copies:
        c.start()

    def wait(*which):
        for i in which:
            copies[i].wait()

    return wait


def step_kernel(count, hidx, ct, snd, rcv, nf_h, gz_h, pw_h, ein_h, ef_h, ebias_h, eout_h, nin_h,
                nbias_h, nout_h, rw_h, cin_h, cbias_h, cout_h, prol_h, ge_h,
                w_out, b_out, nr_out, dn_out, def_out, en_out,
                nf, gz, pw, ein, ef, ebias, eout, nin, nbias, nout, rw, cin, cbias, cout, prol, ge, ls,
                own, halo, spart, sland, xs, xr, he, ds, enb, acc, agg,
                y, hn, dsn, part, cland, gc_own, gc, q_own, q_all, gagg, gyn, ssum, wacc, wbuf, gueb_s,
                defb, dh, hland, bias0, bias1, bl1, bl2,
                fs, fr, sss, ssr, css, csr, cgs, cgr, qs, qr, hs, hr, c1s, c1r, c2s, c2r, outs, *sums):
    r, g = here()
    ready = greet(r, g, ALL_PEERS)
    half_way = len(sums) // 2
    early = Total(r, g, wbuf, w_out, W_LATE, *EARLY, sums[:half_way])
    late = Total(r, g, wbuf, w_out, 0, *LATE, sums[half_way:])
    loaded = fetch(
        [(nf_h, nf), (gz_h, gz), (pw_h, pw), (ein_h, ein), (ef_h, ef), (ebias_h, ebias), (eout_h, eout),
         (nin_h, nin), (nbias_h, nbias), (nout_h, nout), (rw_h, rw), (cin_h, cin), (cbias_h, cbias),
         (cout_h, cout), (prol_h, prol), (ge_h, ge)],
        ls,
    )
    per = SUB // 128

    def grp(k):
        return (r, lax.rem(g + k, NG))

    def row(k):
        return (lax.rem(r + k, NR), g)

    def bias_of(ref):
        return ref[...].astype(F32).reshape(1, H)

    def swap_halo(src, dst, send, recv, sign):
        return [
            remote(
                src.at[pl.ds(32 * d, 32)], dst.at[pl.ds(32 * d, 32)], send.at[d], recv.at[d],
                shifted(r, g, sign * dr, sign * dg),
            )
            for d, (dr, dg) in enumerate(OFFSETS)
        ]

    def blank_outside(buf, sign):
        for d, (dr, dg) in enumerate(OFFSETS):
            got = buf[32 * d : 32 * d + 32]
            buf[32 * d : 32 * d + 32] = jnp.where(
                inside(r, g, sign * dr, sign * dg), got, jnp.zeros_like(got)
            )

    def by_block(fn):
        def body(step, carry):
            at8 = pl.ds(pl.multiple_of(step * (BLK // 128), BLK // 128), BLK // 128)
            fn(step, at8)
            return carry

        lax.fori_loop(0, EF // BLK, body, 0)

    def sub(step, h):
        at = pl.ds(pl.multiple_of(step * BLK + h * SUB, SUB), SUB)
        return at, slice(h * per, (h + 1) * per), step * BLK + h * SUB

    pick = halo_pick(hidx[...], 0, NF)
    loaded(0)
    own[...] = mm(pick, nf[...]).astype(BF)
    ready()
    there = swap_halo(own, halo, fs, fr, 1)
    for c in there:
        c.start()
    loaded(1, 2)
    spart[...] = mm(hot_rows(ct[...], 0, GC, pw[...].astype(F32)), gz[...]).astype(BF)
    scat_s = scatter_grp(r, g, spart, sland, sss, ssr, NC)
    over(NG, lambda k: scat_s(k).start())

    def gather(step, at8):
        snd_t, rcv_t = jnp.transpose(snd[at8]), jnp.transpose(rcv[at8])
        for h in range(BLK // SUB):
            at, lanes, _ = sub(step, h)
            xs[at] = mm(hot_cols(snd_t[:, lanes], 0, NF), nf[...]).astype(BF)
            xr[at] = mm(hot_cols(rcv_t[:, lanes], 0, NF), nf[...]).astype(BF)

    by_block(gather)
    acc[...] = jnp.zeros_like(acc)
    loaded(3, 4, 5, 6)
    for c in there:
        c.wait()
    blank_outside(halo, -1)

    def keep_en(step):
        at = pl.ds(pl.multiple_of(step * BLK, BLK), BLK)
        return pltpu.make_async_copy(enb.at[at], en_out.at[at], outs.at[step])

    def forward(step, at8):
        snd_t, rcv8 = jnp.transpose(snd[at8]), rcv[at8]
        for h in range(BLK // SUB):
            at, lanes, first = sub(step, h)
            x = ef[at]
            x_s = xs[at] + mm(hot_cols(snd_t[:, lanes], NF, 256), halo[...]).astype(BF)
            xs[at] = x_s
            u = mm(x, ein[0:H]) + mm(x_s, ein[H : 2 * H]) + mm(xr[at], ein[2 * H :]) + bias_of(ebias)
            s, slope = silu_parts(u)
            hidden = s.astype(BF)
            he[at] = hidden
            ds[at] = slope.astype(BF)
            m = mask_of(count[0], first, SUB)
            new = (x.astype(F32) + m * mm(hidden, eout[...])).astype(BF)
            enb[at] = new
            acc[...] += mm(hot_rows(rcv8[lanes], 0, NF), m.astype(BF) * new)
        keep_en(step).start()

    by_block(forward)
    agg[...] = acc[...].astype(BF)

    loaded(7, 8)
    un = mm(nf[...], nin[0:H]) + mm(agg[...], nin[H:]) + bias_of(nbias)
    s, slope = silu_parts(un)
    hn[...] = s.astype(BF)
    dsn[...] = slope.astype(BF)
    loaded(9, 10)
    fresh = nf[...].astype(F32) + mm(hn[...], nout[...])
    y[...] = fresh
    part[...] = mm(hot_rows(ct[...], 0, GC, rw[...].astype(F32)), fresh.astype(BF)).astype(BF)
    scat = scatter_grp(r, g, part, cland, css, csr, NC)
    over(NG, lambda k: scat(k).start())

    loaded(11, 12, 13, 14)
    over(NG, lambda k: scat_s(k).wait())
    total = spart[rows(g, NC)].astype(F32)
    for k in range(NG - 1):
        total += sland[k].astype(F32)
    sb = total.astype(BF)
    gcn = mm_nt(sb, prol[...])
    gcnb = gcn.astype(BF)
    gh = mm_nt(gcnb, cout[...])
    ssum[...] = jnp.zeros_like(ssum)
    wacc[...] = jnp.zeros_like(wacc)
    bias0[...] = jnp.zeros_like(bias0)
    over(NG, lambda k: scat(k).wait())
    c = part[rows(g, NC)].astype(F32)
    for k in range(NG - 1):
        c += cland[k].astype(F32)
    cb = c.astype(BF)
    uc = mm(cb, cin[...]) + bias_of(cbias)
    s, slope = silu_parts(uc)
    hc = s.astype(BF)
    guc = gh * slope
    gucb = guc.astype(BF)
    gco = (gcn + mm_nt(gucb, cin[...])).astype(BF)
    gc_own[...] = gco
    gc[rows(g, NC)] = gco

    def give_gc(k):
        return remote(gc_own, gc.at[rows(g, NC)], cgs.at[k - 1], cgr.at[k - 1], grp(k))

    over(NG, lambda k: give_gc(k).start())
    q = (c + mm(hc, cout[...])).astype(BF)
    q_own[...] = q
    q_all[rows(g, NC)] = q
    wbuf[1792:2048] = mm_tn(cb, gucb).astype(BF)
    wbuf[2048:2304] = mm_tn(hc, gcnb).astype(BF)
    wbuf[2304:2560] = mm_tn(q, sb).astype(BF)
    bias0[2:3] = jnp.sum(guc, axis=0, keepdims=True)
    table = hot_cols(jnp.transpose(ct[...]), 0, GC, jnp.transpose(rw[...].astype(F32)))
    over(NG, lambda k: give_gc(k).wait())

    def give_q(k):
        return remote(q_own, q_all.at[rows(g, NC)], qs.at[k - 1], qr.at[k - 1], grp(k))

    over(NG, lambda k: give_q(k).start())

    gy = gz[...].astype(F32) + mm(table, gc[...])
    gyb = gy.astype(BF)
    gun = mm_nt(gyb, nout[...]) * dsn[...].astype(F32)
    gunb = gun.astype(BF)
    gagg[...] = mm_nt(gunb, nin[H:]).astype(BF)
    gyn[...] = gy + mm_nt(gunb, nin[0:H])
    wbuf[1024:1280] = mm_tn(nf[...], gunb).astype(BF)
    wbuf[1280:1536] = mm_tn(agg[...], gunb).astype(BF)
    wbuf[1536:1792] = mm_tn(hn[...], gyb).astype(BF)
    bias0[1:2] = jnp.sum(gun, axis=0, keepdims=True)
    early.start_one()

    loaded(15)

    def backward(step, at8):
        rcv_t = jnp.transpose(rcv[at8])
        for h in range(BLK // SUB):
            at, lanes, first = sub(step, h)
            m = mask_of(count[0], first, SUB)
            gen = ge[at].astype(F32) + m * mm(hot_cols(rcv_t[:, lanes], 0, NF), gagg[...])
            gm = (m * gen).astype(BF)
            gue = mm_nt(gm, eout[...]) * ds[at].astype(F32)
            gueb = gue.astype(BF)
            gueb_s[at] = gueb
            defb[at] = gen.astype(BF)
            wacc[0:H] += mm_tn(ef[at], gueb)
            wacc[H : 2 * H] += mm_tn(xs[at], gueb)
            wacc[2 * H : 3 * H] += mm_tn(xr[at], gueb)
            wacc[3 * H :] += mm_tn(he[at], gm)
            bias0[0:1] += jnp.sum(gue, axis=0, keepdims=True)

    by_block(backward)
    wbuf[0 : 4 * H] = wacc[...].astype(BF)
    late.start_one()

    def one_bias(k):
        return remote(bias0, bl1.at[k - 1], c1s.at[k - 1], c1r.at[k - 1], grp(k))

    def two_bias(k):
        return remote(bias1, bl2.at[k - 1], c2s.at[k - 1], c2r.at[k - 1], row(k))

    over(NG, lambda k: one_bias(k).start())
    early.start_two()

    def keep_def(step):
        at = pl.ds(pl.multiple_of(step * BLK, BLK), BLK)
        return pltpu.make_async_copy(defb.at[at], def_out.at[at], outs.at[EF // BLK + step])

    def scatter(step, at8):
        snd8, rcv8 = snd[at8], rcv[at8]
        for h in range(BLK // SUB):
            at, lanes, _ = sub(step, h)
            gueb = gueb_s[at]
            ssum[0:NX] += mm(hot_rows(snd8[lanes], 0, NX), gueb)
            ssum[NX:] += mm(hot_rows(rcv8[lanes], 0, NF), gueb)
            defb[at] = (defb[at].astype(F32) + mm_nt(gueb, ein[0:H])).astype(BF)
        keep_def(step).start()

    by_block(scatter)
    sums_b = ssum[...].astype(BF)
    dh[...] = mm_nt(sums_b[NF:NX], ein[H : 2 * H]).astype(BF)
    back = swap_halo(dh, hland, hs, hr, -1)
    for b in back:
        b.start()
    late.start_two()
    early.start_three()
    over(NG, lambda k: one_bias(k).wait())
    total = bias0[...]
    for k in range(NG - 1):
        total += bl1[k]
    bias1[...] = total
    over(NR, lambda k: two_bias(k).start())
    gyn[...] += mm_nt(sums_b[0:NF], ein[H : 2 * H]) + mm_nt(sums_b[NX:], ein[2 * H :])
    late.start_three()
    early.start_four()
    over(NG, lambda k: give_q(k).wait())
    ptable = hot_cols(jnp.transpose(ct[...]), 0, GC, jnp.transpose(pw[...].astype(F32)))
    y[...] += mm(ptable, mm(q_all[...], prol[...]).astype(BF))
    last = 2 * (EF // BLK)
    keep_nr = pltpu.make_async_copy(y, nr_out, outs.at[last])
    keep_nr.start()
    for b in back:
        b.wait()
    blank_outside(hland, 1)
    late.start_four()
    gyn[...] += mm_tn(halo_pick(hidx[...], 0, NF), hland[...])
    keep_dn = pltpu.make_async_copy(gyn, dn_out, outs.at[last + 1])
    keep_dn.start()
    over(NR, lambda k: two_bias(k).wait())
    total = bias1[...]
    for k in range(NR - 1):
        total += bl2[k]
    b_out[...] = total
    early.finish()
    for step in range(EF // BLK):
        keep_en(step).wait()
        keep_def(step).wait()
    keep_nr.wait()
    keep_dn.wait()
    late.finish()


PARTS = 4


def result_kernel(b, nr, dn, de, en, w_ein, w_eout, w_nin, w_nout, w_cin, w_cout, w_pr,
                  o_eb, o_nb, o_cb, nr_out, dnf_out, def_out, en_out,
                  o_ein, o_eout, o_nin, o_nout, o_cin, o_cout, o_pr):
    @pl.when(pl.program_id(0) == 0)
    def _():
        o_eb[...] = b[0:1].reshape(H)
        o_nb[...] = b[1:2].reshape(H)
        o_cb[...] = b[2:3].reshape(H)

    for dst, src in ((nr_out, nr), (dnf_out, dn), (def_out, de), (en_out, en),
                     (o_ein, w_ein), (o_eout, w_eout), (o_nin, w_nin), (o_nout, w_nout),
                     (o_cin, w_cin), (o_cout, w_cout), (o_pr, w_pr)):
        dst[...] = src[...].astype(F32)


def body(node_feat, edge_feat, senders, receivers, edge_count, halo_index, coarse_target,
         restrict_weight, prolong_weight, edge_in, edge_bias, edge_out, node_in, node_bias, node_out,
         coarse_in, coarse_bias, coarse_out, prolong, grad_nodes, grad_edges):
    snd = senders.reshape(EF // 128, 128)
    rcv = receivers.reshape(EF // 128, 128)
    ct = coarse_target.reshape(NF // 128, 128)
    rw = restrict_weight.reshape(NF // 128, 128)
    pw = prolong_weight.reshape(NF // 128, 128)
    hidx = halo_index.reshape(8, 32)

    def shape(dims, dtype=BF):
        return jax.ShapeDtypeStruct(dims, dtype)

    def sems(*sizes):
        return [pltpu.SemaphoreType.DMA((n,)) for n in sizes]

    def whole(n):
        return [pl.BlockSpec(memory_space=pltpu.VMEM)] * n

    def far(n):
        return [pl.BlockSpec(memory_space=pl.ANY)] * n

    def vmem(*dims, dtype=BF):
        return pltpu.VMEM(dims, dtype)

    blocks = EF // BLK
    w_all, b_all, nr, dn, de, en = pl.pallas_call(
        step_kernel,
        out_shape=[
            shape((WROWS, H)), shape((8, H), F32), shape((NF, H), F32), shape((NF, H), F32),
            shape((EF, H)), shape((EF, H)),
        ],
        in_specs=[pl.BlockSpec(memory_space=pltpu.SMEM)] + whole(4) + far(16),
        out_specs=whole(2) + far(4),
        scratch_shapes=[
            vmem(NF, H), vmem(NF, H), vmem(8, 128), vmem(768, H), vmem(EF, H), vmem(H), vmem(H, H),
            vmem(512, H), vmem(H), vmem(H, H), vmem(8, 128), vmem(H, H), vmem(H), vmem(H, H), vmem(H, H),
            vmem(EF, H),
        ]
        + sems(16)
        + [
            vmem(256, H), vmem(256, H), vmem(GC, H), vmem(NG - 1, NC, H), vmem(EF, H), vmem(EF, H),
            vmem(EF, H), vmem(EF, H), vmem(EF, H), vmem(NF, H, dtype=F32), vmem(NF, H),
        ]
        + [
            vmem(NF, H, dtype=F32), vmem(NF, H), vmem(NF, H), vmem(GC, H), vmem(NG - 1, NC, H),
            vmem(NC, H), vmem(GC, H), vmem(NC, H), vmem(GC, H), vmem(NF, H), vmem(NF, H, dtype=F32),
            vmem(NT, H, dtype=F32), vmem(1024, H, dtype=F32), vmem(WROWS, H), vmem(EF, H), vmem(EF, H),
            vmem(256, H), vmem(256, H), vmem(8, H, dtype=F32), vmem(8, H, dtype=F32),
            vmem(NG - 1, 8, H, dtype=F32), vmem(NR - 1, 8, H, dtype=F32),
        ]
        + sems(8, 8, 7, 7, 7, 7, 7, 7, 7, 7, 8, 8, 7, 7, 15, 15, 2 * blocks + 2)
        + Total.scratch(*EARLY)
        + Total.scratch(*LATE),
        compiler_params=pltpu.CompilerParams(
            collective_id=0, has_side_effects=True, vmem_limit_bytes=LIMIT * MIB
        ),
        name="step",
    )(edge_count, hidx, ct, snd, rcv, node_feat, grad_nodes, pw, edge_in, edge_feat, edge_bias, edge_out,
      node_in, node_bias, node_out, rw, coarse_in, coarse_bias, coarse_out, prolong, grad_edges)

    def fixed(*dims):
        return pl.BlockSpec(dims, lambda i: (0,) * len(dims))

    def piece(size, start=0):
        return pl.BlockSpec((size // PARTS, H), lambda i: (start * PARTS // size + i, 0))

    sizes = (768, 256, 512, 256, 256, 256, 256)
    starts = (0, 768, 1024, 1536, 1792, 2048, 2304)
    big = [piece(NF), piece(NF), piece(EF), piece(EF)]
    (g_eb, g_nb, g_cb, node_result, d_node_feat, d_edge_feat, edge_new, g_ein, g_eout, g_nin, g_nout,
     g_cin, g_cout, g_pr) = pl.pallas_call(
        result_kernel,
        grid=(PARTS,),
        out_shape=[shape((H,), F32)] * 3
        + [shape((n, H), F32) for n in (NF, NF, EF, EF) + sizes],
        in_specs=[fixed(8, H)] + big + [piece(n, at) for n, at in zip(sizes, starts)],
        out_specs=[fixed(H)] * 3 + big + [piece(n) for n in sizes],
        compiler_params=pltpu.CompilerParams(
            dimension_semantics=("arbitrary",), vmem_limit_bytes=LIMIT * MIB
        ),
        name="results",
    )(b_all, nr, dn, de, en, *[w_all] * 7)
    return (node_result, edge_new, d_node_feat, d_edge_feat, g_ein, g_eb, g_eout, g_nin, g_nb, g_nout,
            g_cin, g_cb, g_cout, g_pr)


def solution(mesh):
    wide = P(("row", "grp"), None)
    line = P(("row", "grp"))
    in_specs = (
        (wide, wide, line, line, line, P(("row", "grp"), None, None), line, line, line)
        + (P(),) * 10
        + (wide, wide)
    )
    out_specs = (wide,) * 4 + (P(),) * 10
    return jax.shard_map(body, mesh=mesh, in_specs=in_specs, out_specs=out_specs, check_vma=False)
```

time: 114 us -> 92.1 us (0.81)
  Pallas kernels: 109 us -> 90.5 us
  local copies, waits for them, and re-layouts: 3.66 us -> 0 us
    pallas_call x4 -> x2, Pallas kernels: 109 us -> 90.5 us  [the longest x1 82 us: body(): pl.pallas_call(step_kernel, out_shape=[shape((WROWS, H)), shape((8, H), F...]
    reshape x3 -> x0, local copies, waits for them, and re-layouts: 3.66 us -> none  [body(): v.reshape(1, H)]
where the time goes in v3:
time: 92.1 us; the launch traced here: 91.8 us
  Pallas kernels  90.5 us (98%)
  between operations  1.31 us (1%)
    pallas_call x1, Pallas kernels, body(): pl.pallas_call(step_kernel, out_shape=[shape((WROWS, H)), shape((8, H), F...  82 us
    pallas_call x1, Pallas kernels, body(): pl.pallas_call(result_kernel, grid=(PARTS,), out_shape=[shape((H,), F32)]...  8.45 us

profile of v3, /device:TPU:1, one launch (start us, length us, event | category | flops | bytes accessed | tf_op | source)
XLA Modules:
  0.0 91.8 jit_solution(12740834489883447231)
XLA Ops:
  1.3 82.0 %step.1 = (bf16[2560,256]{1,0:T(8,128)(2,1)}, f32[8,256]{1,0:T(8,128)}, f32[1024,256]{1,0:T(8,128)}, f32[1024,256]{1,0:T(8,128)}, bf16[4096,256]{1,0:T(8,128)(2,1)}, /*index=5*/bf16[4096,256]{1,0:T(8,128)(2,1)}) custom-call(s32[1]{0:T(128)S(6)} %copy.35.count, s32[8,32]{1,0:T(8,128)} %bitcast.8, s32[8,128]{1,0:T(8,128)} %bitcast.9, s32[32,128]{1,0:T(8,128)} %bitcast.6, ...), custom_call_target="tpu_custom_call" | custom-call | tf_op jit(solution)/shard_map/step/pallas_call | solution.py:598
  83.3 8.5 %results.1 = (f32[256]{0:T(256)}, f32[256]{0:T(256)}, f32[256]{0:T(256)}, f32[1024,256]{1,0:T(8,128)}, f32[1024,256]{1,0:T(8,128)}, /*index=5*/f32[4096,256]{1,0...) custom-call(f32[8,256]{1,0:T(8,128)} %get-tuple-element.34.b, ...), custom_call_target="tpu_custom_call" | custom-call | tf_op jit(solution)/shard_map/results/pallas_call | solution.py:643

commit v4 on v3

--- a/solution.py
+++ b/solution.py
@@ -110,6 +110,10 @@
     )
 
 
+def both(buf, send, recv, place):
+    remote(buf, buf, send, recv, place).wait()
+
+
 def rows(start, size):
     return pl.ds(pl.multiple_of(start * size, size), size)
 
@@ -124,7 +128,7 @@
 def scatter_grp(r, g, part, land, send, recv, size):
     def copy(k):
         t = lax.rem(g + k, NG)
-        return remote(part.at[rows(t, size)], land.at[k - 1], send.at[k - 1], recv.at[k - 1], (r, t))
+        return remote(part.at[rows(t, size)], land.at[k - 1], send.at[0], recv.at[0], (r, t))
 
     return copy
 
@@ -149,7 +153,6 @@
     @staticmethod
     def scratch(na, nb):
         ra, rb = na // NG, nb // NR
-        counts = [NG - 1, NR - 1, NR - 1, NG - 1, NR - 1, NG - 1, NG - 1, NR - 1]
         return [
             pltpu.VMEM((NG - 1, ra, H), BF),
             pltpu.VMEM((NR - 1, rb, H), BF),
@@ -161,7 +164,7 @@
             pltpu.VMEM((rb // 4, 128), F32),
             pltpu.VMEM((ra, H), F32),
             pltpu.VMEM((rb, H), F32),
-        ] + [pltpu.SemaphoreType.DMA((n,)) for n in counts for _ in range(2)]
+        ] + [pltpu.SemaphoreType.DMA((1,))] * 16
 
     def block_a(self, t):
         return pl.ds(pl.multiple_of(self.base + t * self.ra, 16), self.ra)
@@ -171,7 +174,10 @@
 
     def copy(self, stage, src, dst, k, place):
         send, recv = self.sems[2 * stage], self.sems[2 * stage + 1]
-        return remote(src, dst, send.at[k - 1], recv.at[k - 1], place)
+        return remote(src, dst, send.at[0], recv.at[0], place)
+
+    def wait(self, stage, buf):
+        both(buf, self.sems[2 * stage].at[0], self.sems[2 * stage + 1].at[0], (self.r, self.g))
 
     def grp(self, k):
         return lax.rem(self.g + k, NG)
@@ -218,13 +224,13 @@
         over(NG, lambda k: self.one_a(k).start())
 
     def start_two(self):
-        over(NR, lambda k: self.one_b(k).wait())
+        self.wait(1, self.b1)
         total = self.wbuf[self.block_b(self.r)].astype(F32)
         for k in range(NR - 1):
             total += self.b1[k].astype(F32)
         self.acc_b[...] = total
         over(NG, lambda k: self.two_b(k).start())
-        over(NG, lambda k: self.one_a(k).wait())
+        self.wait(0, self.a1)
         total = self.wbuf[self.block_a(self.g)].astype(F32)
         for k in range(NG - 1):
             total += self.a1[k].astype(F32)
@@ -232,7 +238,7 @@
         over(NR, lambda k: self.two_a(k).start())
 
     def start_three(self):
-        over(NG, lambda k: self.two_b(k).wait())
+        self.wait(3, self.b2)
         at = rows(self.g // 2, self.pb), lanes_half(self.g)
         total = self.acc_b[at]
         for k in range(NG - 1):
@@ -240,7 +246,7 @@
         self.mine_b[...] = total
         self.all_b[at] = total
         over(NG, lambda k: self.three_b(k).start())
-        over(NR, lambda k: self.two_a(k).wait())
+        self.wait(2, self.a2)
         at = rows(self.r // 2, self.pa), lanes_half(self.r)
         total = self.acc_a[at]
         for k in range(NR - 1):
@@ -250,16 +256,16 @@
         over(NR, lambda k: self.three_a(k).start())
 
     def start_four(self):
-        over(NG, lambda k: self.three_b(k).wait())
+        self.wait(5, self.b2)
         self.out[self.block_b(self.r)] = self.all_b[...].astype(BF)
         over(NR, lambda k: self.four_b(k).start())
-        over(NR, lambda k: self.three_a(k).wait())
+        self.wait(4, self.a2)
         self.out[self.block_a(self.g)] = self.all_a[...].astype(BF)
         over(NG, lambda k: self.four_a(k).start())
 
     def finish(self):
-        over(NR, lambda k: self.four_b(k).wait())
-        over(NG, lambda k: self.four_a(k).wait())
+        self.wait(7, self.b1)
+        self.wait(6, self.a1)
 
 
 LATE = (512, 512)
@@ -316,7 +322,7 @@
     def swap_halo(src, dst, send, recv, sign):
         return [
             remote(
-                src.at[pl.ds(32 * d, 32)], dst.at[pl.ds(32 * d, 32)], send.at[d], recv.at[d],
+                src.at[pl.ds(32 * d, 32)], dst.at[pl.ds(32 * d, 32)], send.at[0], recv.at[0],
                 shifted(r, g, sign * dr, sign * dg),
             )
             for d, (dr, dg) in enumerate(OFFSETS)
@@ -363,8 +369,7 @@
     by_block(gather)
     acc[...] = jnp.zeros_like(acc)
     loaded(3, 4, 5, 6)
-    for c in there:
-        c.wait()
+    both(halo, fs.at[0], fr.at[0], (r, g))
     blank_outside(halo, -1)
 
     def keep_en(step):
@@ -405,7 +410,7 @@
     over(NG, lambda k: scat(k).start())
 
     loaded(11, 12, 13, 14)
-    over(NG, lambda k: scat_s(k).wait())
+    both(sland, sss.at[0], ssr.at[0], (r, g))
     total = spart[rows(g, NC)].astype(F32)
     for k in range(NG - 1):
         total += sland[k].astype(F32)
@@ -416,7 +421,7 @@
     ssum[...] = jnp.zeros_like(ssum)
     wacc[...] = jnp.zeros_like(wacc)
     bias0[...] = jnp.zeros_like(bias0)
-    over(NG, lambda k: scat(k).wait())
+    both(cland, css.at[0], csr.at[0], (r, g))
     c = part[rows(g, NC)].astype(F32)
     for k in range(NG - 1):
         c += cland[k].astype(F32)
@@ -431,7 +436,7 @@
     gc[rows(g, NC)] = gco
 
     def give_gc(k):
-        return remote(gc_own, gc.at[rows(g, NC)], cgs.at[k - 1], cgr.at[k - 1], grp(k))
+        return remote(gc_own, gc.at[rows(g, NC)], cgs.at[0], cgr.at[0], grp(k))
 
     over(NG, lambda k: give_gc(k).start())
     q = (c + mm(hc, cout[...])).astype(BF)
@@ -442,10 +447,10 @@
     wbuf[2304:2560] = mm_tn(q, sb).astype(BF)
     bias0[2:3] = jnp.sum(guc, axis=0, keepdims=True)
     table = hot_cols(jnp.transpose(ct[...]), 0, GC, jnp.transpose(rw[...].astype(F32)))
-    over(NG, lambda k: give_gc(k).wait())
+    both(cland, cgs.at[0], cgr.at[0], (r, g))
 
     def give_q(k):
-        return remote(q_own, q_all.at[rows(g, NC)], qs.at[k - 1], qr.at[k - 1], grp(k))
+        return remote(q_own, q_all.at[rows(g, NC)], qs.at[0], qr.at[0], grp(k))
 
     over(NG, lambda k: give_q(k).start())
 
@@ -485,10 +490,10 @@
     late.start_one()
 
     def one_bias(k):
-        return remote(bias0, bl1.at[k - 1], c1s.at[k - 1], c1r.at[k - 1], grp(k))
+        return remote(bias0, bl1.at[k - 1], c1s.at[0], c1r.at[0], grp(k))
 
     def two_bias(k):
-        return remote(bias1, bl2.at[k - 1], c2s.at[k - 1], c2r.at[k - 1], row(k))
+        return remote(bias1, bl2.at[k - 1], c2s.at[0], c2r.at[0], row(k))
 
     over(NG, lambda k: one_bias(k).start())
     early.start_two()
@@ -515,7 +520,7 @@
         b.start()
     late.start_two()
     early.start_three()
-    over(NG, lambda k: one_bias(k).wait())
+    both(bl1, c1s.at[0], c1r.at[0], (r, g))
     total = bias0[...]
     for k in range(NG - 1):
         total += bl1[k]
@@ -524,20 +529,19 @@
     gyn[...] += mm_nt(sums_b[0:NF], ein[H : 2 * H]) + mm_nt(sums_b[NX:], ein[2 * H :])
     late.start_three()
     early.start_four()
-    over(NG, lambda k: give_q(k).wait())
+    both(cland, qs.at[0], qr.at[0], (r, g))
     ptable = hot_cols(jnp.transpose(ct[...]), 0, GC, jnp.transpose(pw[...].astype(F32)))
     y[...] += mm(ptable, mm(q_all[...], prol[...]).astype(BF))
     last = 2 * (EF // BLK)
     keep_nr = pltpu.make_async_copy(y, nr_out, outs.at[last])
     keep_nr.start()
-    for b in back:
-        b.wait()
+    both(hland, hs.at[0], hr.at[0], (r, g))
     blank_outside(hland, 1)
     late.start_four()
     gyn[...] += mm_tn(halo_pick(hidx[...], 0, NF), hland[...])
     keep_dn = pltpu.make_async_copy(gyn, dn_out, outs.at[last + 1])
     keep_dn.start()
-    over(NR, lambda k: two_bias(k).wait())
+    both(bl2, c2s.at[0], c2r.at[0], (r, g))
     total = bias1[...]
     for k in range(NR - 1):
         total += bl2[k]
@@ -551,22 +555,48 @@
     late.finish()
 
 
-PARTS = 4
-
-
-def result_kernel(b, nr, dn, de, en, w_ein, w_eout, w_nin, w_nout, w_cin, w_cout, w_pr,
-                  o_eb, o_nb, o_cb, nr_out, dnf_out, def_out, en_out,
-                  o_ein, o_eout, o_nin, o_nout, o_cin, o_cout, o_pr):
-    @pl.when(pl.program_id(0) == 0)
-    def _():
-        o_eb[...] = b[0:1].reshape(H)
-        o_nb[...] = b[1:2].reshape(H)
-        o_cb[...] = b[2:3].reshape(H)
-
-    for dst, src in ((nr_out, nr), (dnf_out, dn), (def_out, de), (en_out, en),
-                     (o_ein, w_ein), (o_eout, w_eout), (o_nin, w_nin), (o_nout, w_nout),
-                     (o_cin, w_cin), (o_cout, w_cout), (o_pr, w_pr)):
-        dst[...] = src[...].astype(F32)
+SIZES = (768, 256, 512, 256, 256, 256, 256)
+CHUNK = 2048
+
+
+def result_kernel(b, nr_h, dn_h, de_h, en_h, w_h, *refs):
+    biases, big, mats = refs[0:3], refs[3:7], refs[7:14]
+    nr, dn, de, en, w, wide_de, wide_en, wide_w, in_sem, out_sem = refs[14:]
+    chunks = [pl.ds(c * CHUNK, CHUNK) for c in range(EF // CHUNK)]
+    arriving, leaving = [], []
+
+    def bring(src, dst):
+        arriving.append(pltpu.make_async_copy(src, dst, in_sem.at[len(arriving)]))
+        arriving[-1].start()
+        return arriving[-1]
+
+    def leave(src, dst):
+        leaving.append(pltpu.make_async_copy(src, dst, out_sem.at[len(leaving)]))
+        leaving[-1].start()
+
+    edges = []
+    for at in chunks:
+        for src, mid, wide, dst in ((en_h, en, wide_en, big[0]), (de_h, de, wide_de, big[1])):
+            edges.append((bring(src.at[at], mid.at[at]), mid, wide, dst, at))
+    nodes = [(bring(src, mid), mid, dst) for src, mid, dst in ((nr_h, nr, big[2]), (dn_h, dn, big[3]))]
+    w_here = bring(w_h, w)
+    for here_, mid, wide, dst, at in edges:
+        here_.wait()
+        wide[at] = mid[at].astype(F32)
+        leave(wide.at[at], dst.at[at])
+    for here_, mid, dst in nodes:
+        here_.wait()
+        leave(mid, dst)
+    w_here.wait()
+    first = 0
+    for dst, size in zip(mats, SIZES):
+        wide_w[first : first + size] = w[first : first + size].astype(F32)
+        leave(wide_w.at[pl.ds(first, size)], dst)
+        first += size
+    for i, dst in enumerate(biases):
+        dst[...] = b[i : i + 1].reshape(H)
+    for c in leaving:
+        c.wait()
 
 
 def body(node_feat, edge_feat, senders, receivers, edge_count, halo_index, coarse_target,
@@ -620,7 +650,7 @@
             vmem(256, H), vmem(256, H), vmem(8, H, dtype=F32), vmem(8, H, dtype=F32),
             vmem(NG - 1, 8, H, dtype=F32), vmem(NR - 1, 8, H, dtype=F32),
         ]
-        + sems(8, 8, 7, 7, 7, 7, 7, 7, 7, 7, 8, 8, 7, 7, 15, 15, 2 * blocks + 2)
+        + sems(*[1] * 16, 2 * blocks + 2)
         + Total.scratch(*EARLY)
         + Total.scratch(*LATE),
         compiler_params=pltpu.CompilerParams(
@@ -630,28 +660,21 @@
     )(edge_count, hidx, ct, snd, rcv, node_feat, grad_nodes, pw, edge_in, edge_feat, edge_bias, edge_out,
       node_in, node_bias, node_out, rw, coarse_in, coarse_bias, coarse_out, prolong, grad_edges)
 
-    def fixed(*dims):
-        return pl.BlockSpec(dims, lambda i: (0,) * len(dims))
-
-    def piece(size, start=0):
-        return pl.BlockSpec((size // PARTS, H), lambda i: (start * PARTS // size + i, 0))
-
-    sizes = (768, 256, 512, 256, 256, 256, 256)
-    starts = (0, 768, 1024, 1536, 1792, 2048, 2304)
-    big = [piece(NF), piece(NF), piece(EF), piece(EF)]
-    (g_eb, g_nb, g_cb, node_result, d_node_feat, d_edge_feat, edge_new, g_ein, g_eout, g_nin, g_nout,
-     g_cin, g_cout, g_pr) = pl.pallas_call(
+    chunks = EF // CHUNK
+    g_eb, g_nb, g_cb, edge_new, d_edge_feat, node_result, d_node_feat, *mats = pl.pallas_call(
         result_kernel,
-        grid=(PARTS,),
-        out_shape=[shape((H,), F32)] * 3
-        + [shape((n, H), F32) for n in (NF, NF, EF, EF) + sizes],
-        in_specs=[fixed(8, H)] + big + [piece(n, at) for n, at in zip(sizes, starts)],
-        out_specs=[fixed(H)] * 3 + big + [piece(n) for n in sizes],
-        compiler_params=pltpu.CompilerParams(
-            dimension_semantics=("arbitrary",), vmem_limit_bytes=LIMIT * MIB
-        ),
+        out_shape=[shape((H,), F32)] * 3 + [shape((n, H), F32) for n in (EF, EF, NF, NF) + SIZES],
+        in_specs=whole(1) + far(5),
+        out_specs=whole(3) + far(11),
+        scratch_shapes=[
+            vmem(NF, H, dtype=F32), vmem(NF, H, dtype=F32), vmem(EF, H), vmem(EF, H), vmem(WROWS, H),
+            vmem(EF, H, dtype=F32), vmem(EF, H, dtype=F32), vmem(WROWS, H, dtype=F32),
+        ]
+        + sems(2 * chunks + 3, 2 * chunks + 9),
+        compiler_params=pltpu.CompilerParams(vmem_limit_bytes=LIMIT * MIB),
         name="results",
-    )(b_all, nr, dn, de, en, *[w_all] * 7)
+    )(b_all, nr, dn, de, en, w_all)
+    g_ein, g_eout, g_nin, g_nout, g_cin, g_cout, g_pr = mats
     return (node_result, edge_new, d_node_feat, d_edge_feat, g_ein, g_eb, g_eout, g_nin, g_nb, g_nout,
             g_cin, g_cb, g_cout, g_pr)
 

time: 92.1 us -> 87.5 us (0.950)
  Pallas kernels: 90.5 us -> 86 us
    pallas_call x1, Pallas kernels: 82 us -> 77.7 us  [body(): pl.pallas_call(step_kernel, out_shape=[shape((WROWS, H)), shape((8, H), F...]
where the time goes in v4:
time: 87.5 us; the launch traced here: 87.3 us
  Pallas kernels  86 us (98%)
  between operations  1.31 us (1%)
    pallas_call x1, Pallas kernels, body(): pl.pallas_call(step_kernel, out_shape=[shape((WROWS, H)), shape((8, H), F...  77.7 us
    pallas_call x1, Pallas kernels, body(): pl.pallas_call(result_kernel, out_shape=[shape((H,), F32)] * 3 + [shape((...  8.25 us

profile of v4, /device:TPU:1, one launch (start us, length us, event | category | flops | bytes accessed | tf_op | source)
XLA Modules:
  0.0 87.3 jit_solution(139015616236198865)
XLA Ops:
  1.3 77.7 %step.1 = (bf16[2560,256]{1,0:T(8,128)(2,1)}, f32[8,256]{1,0:T(8,128)}, f32[1024,256]{1,0:T(8,128)}, f32[1024,256]{1,0:T(8,128)}, bf16[4096,256]{1,0:T(8,128)(2,1)}, /*index=5*/bf16[4096,256]{1,0:T(8,128)(2,1)}) custom-call(s32[1]{0:T(128)S(6)} %copy.35.count, s32[8,32]{1,0:T(8,128)} %bitcast.8, s32[8,128]{1,0:T(8,128)} %bitcast.9, s32[32,128]{1,0:T(8,128)} %bitcast.6, ...), custom_call_target="tpu_custom_call" | custom-call | tf_op jit(solution)/shard_map/step/pallas_call | solution.py:628
  79.0 8.2 %results.1 = (f32[256]{0:T(256)}, f32[256]{0:T(256)}, f32[256]{0:T(256)}, f32[4096,256]{1,0:T(8,128)}, f32[4096,256]{1,0:T(8,128)}, /*index=5*/f32[1024,256]{1,0...) custom-call(f32[8,256]{1,0:T(8,128)} %get-tuple-element.34.b, ...), custom_call_target="tpu_custom_call" | custom-call | tf_op jit(solution)/shard_map/results/pallas_call | solution.py:664

commit v5 on v4

--- a/solution.py
+++ b/solution.py
@@ -18,8 +18,8 @@
 NT = NX + NF
 GC = 512
 NC = 64
-BLK = 1024
-SUB = 512
+BLK = 2048
+SUB = 1024
 MIB = 1024 * 1024
 LIMIT = 60
 
@@ -133,7 +133,7 @@
     return copy
 
 
-W_LATE, W_EARLY = 1024, 1536
+W_LATE, W_EARLY = 768, 1792
 WROWS = W_LATE + W_EARLY
 
 
@@ -146,9 +146,9 @@
         self.r, self.g, self.wbuf, self.out = r, g, wbuf, out
         self.base, self.na, self.nb = base, na, nb
         self.ra, self.rb = na // NG, nb // NR
-        self.pa, self.pb = self.ra // 8, self.rb // 4
-        (self.a1, self.b1, self.acc_a, self.acc_b, self.a2, self.b2, self.mine_a, self.mine_b,
-         self.all_a, self.all_b, *self.sems) = scratch
+        self.pa = self.ra // 8
+        (self.a1, self.b1, self.acc_a, self.mine_b, self.a2, self.b2, self.mine_a, self.all_a,
+         *self.sems) = scratch
 
     @staticmethod
     def scratch(na, nb):
@@ -157,14 +157,12 @@
             pltpu.VMEM((NG - 1, ra, H), BF),
             pltpu.VMEM((NR - 1, rb, H), BF),
             pltpu.VMEM((ra, H), F32),
-            pltpu.VMEM((rb, H), F32),
+            pltpu.VMEM((rb, H), BF),
             pltpu.VMEM((NR - 1, ra // 8, 128), F32),
-            pltpu.VMEM((NG - 1, rb // 4, 128), F32),
+            pltpu.VMEM((NG, rb, H), BF),
             pltpu.VMEM((ra // 8, 128), F32),
-            pltpu.VMEM((rb // 4, 128), F32),
             pltpu.VMEM((ra, H), F32),
-            pltpu.VMEM((rb, H), F32),
-        ] + [pltpu.SemaphoreType.DMA((1,))] * 16
+        ] + [pltpu.SemaphoreType.DMA((1,))] * 14
 
     def block_a(self, t):
         return pl.ds(pl.multiple_of(self.base + t * self.ra, 16), self.ra)
@@ -172,7 +170,7 @@
     def block_b(self, t):
         return pl.ds(pl.multiple_of(self.base + self.na + t * self.rb, 16), self.rb)
 
-    def copy(self, stage, src, dst, k, place):
+    def copy(self, stage, src, dst, place):
         send, recv = self.sems[2 * stage], self.sems[2 * stage + 1]
         return remote(src, dst, send.at[0], recv.at[0], place)
 
@@ -187,65 +185,52 @@
 
     def one_a(self, k):
         t = self.grp(k)
-        return self.copy(0, self.wbuf.at[self.block_a(t)], self.a1.at[k - 1], k, (self.r, t))
+        self.copy(0, self.wbuf.at[self.block_a(t)], self.a1.at[k - 1], (self.r, t)).start()
 
     def one_b(self, k):
         t = self.row(k)
-        return self.copy(1, self.wbuf.at[self.block_b(t)], self.b1.at[k - 1], k, (t, self.g))
+        self.copy(1, self.wbuf.at[self.block_b(t)], self.b1.at[k - 1], (t, self.g)).start()
 
     def two_a(self, k):
         t = self.row(k)
         src = self.acc_a.at[rows(t // 2, self.pa), lanes_half(t)]
-        return self.copy(2, src, self.a2.at[k - 1], k, (t, self.g))
+        self.copy(2, src, self.a2.at[k - 1], (t, self.g)).start()
 
     def two_b(self, k):
-        t = self.grp(k)
-        src = self.acc_b.at[rows(t // 2, self.pb), lanes_half(t)]
-        return self.copy(3, src, self.b2.at[k - 1], k, (self.r, t))
+        self.copy(3, self.mine_b, self.b2.at[self.g], (self.r, self.grp(k))).start()
 
     def three_a(self, k):
         dst = self.all_a.at[rows(self.r // 2, self.pa), lanes_half(self.r)]
-        return self.copy(4, self.mine_a, dst, k, (self.row(k), self.g))
-
-    def three_b(self, k):
-        dst = self.all_b.at[rows(self.g // 2, self.pb), lanes_half(self.g)]
-        return self.copy(5, self.mine_b, dst, k, (self.r, self.grp(k)))
+        self.copy(4, self.mine_a, dst, (self.row(k), self.g)).start()
 
     def four_a(self, k):
         at = self.out.at[self.block_a(self.g)]
-        return self.copy(6, at, at, k, (self.r, self.grp(k)))
+        self.copy(5, at, at, (self.r, self.grp(k))).start()
 
     def four_b(self, k):
         at = self.out.at[self.block_b(self.r)]
-        return self.copy(7, at, at, k, (self.row(k), self.g))
+        self.copy(6, at, at, (self.row(k), self.g)).start()
 
     def start_one(self):
-        over(NR, lambda k: self.one_b(k).start())
-        over(NG, lambda k: self.one_a(k).start())
+        over(NG, self.one_a)
+        over(NR, self.one_b)
 
     def start_two(self):
         self.wait(1, self.b1)
         total = self.wbuf[self.block_b(self.r)].astype(F32)
         for k in range(NR - 1):
             total += self.b1[k].astype(F32)
-        self.acc_b[...] = total
-        over(NG, lambda k: self.two_b(k).start())
+        self.mine_b[...] = total.astype(BF)
+        self.b2[self.g] = total.astype(BF)
+        over(NG, self.two_b)
         self.wait(0, self.a1)
         total = self.wbuf[self.block_a(self.g)].astype(F32)
         for k in range(NG - 1):
             total += self.a1[k].astype(F32)
         self.acc_a[...] = total
-        over(NR, lambda k: self.two_a(k).start())
+        over(NR, self.two_a)
 
     def start_three(self):
-        self.wait(3, self.b2)
-        at = rows(self.g // 2, self.pb), lanes_half(self.g)
-        total = self.acc_b[at]
-        for k in range(NG - 1):
-            total += self.b2[k]
-        self.mine_b[...] = total
-        self.all_b[at] = total
-        over(NG, lambda k: self.three_b(k).start())
         self.wait(2, self.a2)
         at = rows(self.r // 2, self.pa), lanes_half(self.r)
         total = self.acc_a[at]
@@ -253,23 +238,26 @@
             total += self.a2[k]
         self.mine_a[...] = total
         self.all_a[at] = total
-        over(NR, lambda k: self.three_a(k).start())
+        over(NR, self.three_a)
+        self.wait(3, self.b1.at[pl.ds(0, NG - 1)])
+        total = self.b2[0].astype(F32)
+        for k in range(1, NG):
+            total += self.b2[k].astype(F32)
+        self.out[self.block_b(self.r)] = total.astype(BF)
+        over(NR, self.four_b)
 
     def start_four(self):
-        self.wait(5, self.b2)
-        self.out[self.block_b(self.r)] = self.all_b[...].astype(BF)
-        over(NR, lambda k: self.four_b(k).start())
         self.wait(4, self.a2)
         self.out[self.block_a(self.g)] = self.all_a[...].astype(BF)
-        over(NG, lambda k: self.four_a(k).start())
+        over(NG, self.four_a)
 
     def finish(self):
-        self.wait(7, self.b1)
-        self.wait(6, self.a1)
-
-
-LATE = (512, 512)
-EARLY = (1024, 512)
+        self.wait(6, self.b1)
+        self.wait(5, self.a1)
+
+
+LATE = (512, 256)
+EARLY = (512, 1280)
 
 
 def mask_of(count, start, size):
@@ -294,7 +282,7 @@
                 w_out, b_out, nr_out, dn_out, def_out, en_out,
                 nf, gz, pw, ein, ef, ebias, eout, nin, nbias, nout, rw, cin, cbias, cout, prol, ge, ls,
                 own, halo, spart, sland, xs, xr, he, ds, enb, acc, agg,
-                y, hn, dsn, part, cland, gc_own, gc, q_own, q_all, gagg, gyn, ssum, wacc, wbuf, gueb_s,
+                y, hn, dsn, part, cland, gc_own, gc, q_own, q_all, gagg, gagg_w, gue0, gyn, ssum, wacc, wbuf, gueb_s,
                 defb, dh, hland, bias0, bias1, bl1, bl2,
                 fs, fr, sss, ssr, css, csr, cgs, cgr, qs, qr, hs, hr, c1s, c1r, c2s, c2r, outs, *sums):
     r, g = here()
@@ -418,9 +406,18 @@
     gcn = mm_nt(sb, prol[...])
     gcnb = gcn.astype(BF)
     gh = mm_nt(gcnb, cout[...])
-    ssum[...] = jnp.zeros_like(ssum)
     wacc[...] = jnp.zeros_like(wacc)
     bias0[...] = jnp.zeros_like(bias0)
+    loaded(15)
+
+    def given(step, at8):
+        for h in range(BLK // SUB):
+            at, _, first = sub(step, h)
+            mge = (mask_of(count[0], first, SUB) * ge[at].astype(F32)).astype(BF)
+            gue0[at] = mm_nt(mge, eout[...])
+            wacc[3 * H :] += mm_tn(he[at], mge)
+
+    by_block(given)
     both(cland, css.at[0], csr.at[0], (r, g))
     c = part[rows(g, NC)].astype(F32)
     for k in range(NG - 1):
@@ -447,6 +444,17 @@
     wbuf[2304:2560] = mm_tn(q, sb).astype(BF)
     bias0[2:3] = jnp.sum(guc, axis=0, keepdims=True)
     table = hot_cols(jnp.transpose(ct[...]), 0, GC, jnp.transpose(rw[...].astype(F32)))
+    acc[...] = jnp.zeros_like(acc)
+
+    def he_sums(step, at8):
+        rcv8 = rcv[at8]
+        for h in range(BLK // SUB):
+            at, lanes, first = sub(step, h)
+            mhe = (mask_of(count[0], first, SUB) * he[at].astype(F32)).astype(BF)
+            acc[...] += mm(hot_rows(rcv8[lanes], 0, NF), mhe)
+
+    by_block(he_sums)
+    ssum[...] = jnp.zeros_like(ssum)
     both(cland, cgs.at[0], cgr.at[0], (r, g))
 
     def give_q(k):
@@ -459,6 +467,8 @@
     gun = mm_nt(gyb, nout[...]) * dsn[...].astype(F32)
     gunb = gun.astype(BF)
     gagg[...] = mm_nt(gunb, nin[H:]).astype(BF)
+    gagg_w[...] = mm_nt(gagg[...], eout[...]).astype(BF)
+    wbuf[768:1024] = (wacc[3 * H :] + mm_tn(acc[...].astype(BF), gagg[...])).astype(BF)
     gyn[...] = gy + mm_nt(gunb, nin[0:H])
     wbuf[1024:1280] = mm_tn(nf[...], gunb).astype(BF)
     wbuf[1280:1536] = mm_tn(agg[...], gunb).astype(BF)
@@ -466,50 +476,63 @@
     bias0[1:2] = jnp.sum(gun, axis=0, keepdims=True)
     early.start_one()
 
-    loaded(15)
 
     def backward(step, at8):
         rcv_t = jnp.transpose(rcv[at8])
         for h in range(BLK // SUB):
             at, lanes, first = sub(step, h)
             m = mask_of(count[0], first, SUB)
-            gen = ge[at].astype(F32) + m * mm(hot_cols(rcv_t[:, lanes], 0, NF), gagg[...])
-            gm = (m * gen).astype(BF)
-            gue = mm_nt(gm, eout[...]) * ds[at].astype(F32)
+            gue = (gue0[at] + m * mm(hot_cols(rcv_t[:, lanes], 0, NF), gagg_w[...])) * ds[at].astype(F32)
             gueb = gue.astype(BF)
             gueb_s[at] = gueb
-            defb[at] = gen.astype(BF)
             wacc[0:H] += mm_tn(ef[at], gueb)
             wacc[H : 2 * H] += mm_tn(xs[at], gueb)
             wacc[2 * H : 3 * H] += mm_tn(xr[at], gueb)
-            wacc[3 * H :] += mm_tn(he[at], gm)
             bias0[0:1] += jnp.sum(gue, axis=0, keepdims=True)
 
     by_block(backward)
-    wbuf[0 : 4 * H] = wacc[...].astype(BF)
+    wbuf[0 : 3 * H] = wacc[0 : 3 * H].astype(BF)
     late.start_one()
 
     def one_bias(k):
-        return remote(bias0, bl1.at[k - 1], c1s.at[0], c1r.at[0], grp(k))
+        return remote(bias0, bl1.at[g], c1s.at[0], c1r.at[0], grp(k))
 
     def two_bias(k):
-        return remote(bias1, bl2.at[k - 1], c2s.at[0], c2r.at[0], row(k))
-
+        return remote(bias1, bl2.at[r], c2s.at[0], c2r.at[0], row(k))
+
+    bl1[g] = bias0[...]
     over(NG, lambda k: one_bias(k).start())
-    early.start_two()
 
     def keep_def(step):
         at = pl.ds(pl.multiple_of(step * BLK, BLK), BLK)
         return pltpu.make_async_copy(defb.at[at], def_out.at[at], outs.at[EF // BLK + step])
 
+    def hooked(hooks, step, h):
+        for (at_step, at_h), then in hooks:
+            if at_h == h:
+                pl.when(step == at_step)(then)
+
+    scatter_hooks = (((0, 1), early.start_two), ((1, 1), late.start_two), ((1, 1), early.start_three))
+
     def scatter(step, at8):
         snd8, rcv8 = snd[at8], rcv[at8]
         for h in range(BLK // SUB):
+            hooked(scatter_hooks, step, h)
             at, lanes, _ = sub(step, h)
             gueb = gueb_s[at]
             ssum[0:NX] += mm(hot_rows(snd8[lanes], 0, NX), gueb)
             ssum[NX:] += mm(hot_rows(rcv8[lanes], 0, NF), gueb)
-            defb[at] = (defb[at].astype(F32) + mm_nt(gueb, ein[0:H])).astype(BF)
+
+    widen_hooks = (((0, 1), late.start_three), ((1, 1), early.start_four))
+
+    def edge_grads(step, at8):
+        rcv_t = jnp.transpose(rcv[at8])
+        for h in range(BLK // SUB):
+            hooked(widen_hooks, step, h)
+            at, lanes, first = sub(step, h)
+            m = mask_of(count[0], first, SUB)
+            gen = ge[at].astype(F32) + m * mm(hot_cols(rcv_t[:, lanes], 0, NF), gagg[...])
+            defb[at] = (gen + mm_nt(gueb_s[at], ein[0:H])).astype(BF)
         keep_def(step).start()
 
     by_block(scatter)
@@ -518,32 +541,30 @@
     back = swap_halo(dh, hland, hs, hr, -1)
     for b in back:
         b.start()
-    late.start_two()
-    early.start_three()
-    both(bl1, c1s.at[0], c1r.at[0], (r, g))
-    total = bias0[...]
-    for k in range(NG - 1):
-        total += bl1[k]
-    bias1[...] = total
-    over(NR, lambda k: two_bias(k).start())
+    by_block(edge_grads)
     gyn[...] += mm_nt(sums_b[0:NF], ein[H : 2 * H]) + mm_nt(sums_b[NX:], ein[2 * H :])
-    late.start_three()
-    early.start_four()
     both(cland, qs.at[0], qr.at[0], (r, g))
     ptable = hot_cols(jnp.transpose(ct[...]), 0, GC, jnp.transpose(pw[...].astype(F32)))
     y[...] += mm(ptable, mm(q_all[...], prol[...]).astype(BF))
     last = 2 * (EF // BLK)
     keep_nr = pltpu.make_async_copy(y, nr_out, outs.at[last])
     keep_nr.start()
+    late.start_four()
+    both(bl1.at[pl.ds(0, NG - 1)], c1s.at[0], c1r.at[0], (r, g))
+    total = bl1[0]
+    for k in range(1, NG):
+        total += bl1[k]
+    bias1[...] = total
+    bl2[r] = total
+    over(NR, lambda k: two_bias(k).start())
     both(hland, hs.at[0], hr.at[0], (r, g))
     blank_outside(hland, 1)
-    late.start_four()
     gyn[...] += mm_tn(halo_pick(hidx[...], 0, NF), hland[...])
     keep_dn = pltpu.make_async_copy(gyn, dn_out, outs.at[last + 1])
     keep_dn.start()
-    both(bl2, c2s.at[0], c2r.at[0], (r, g))
-    total = bias1[...]
-    for k in range(NR - 1):
+    both(bl2.at[pl.ds(0, NR - 1)], c2s.at[0], c2r.at[0], (r, g))
+    total = bl2[0]
+    for k in range(1, NR):
         total += bl2[k]
     b_out[...] = total
     early.finish()
@@ -645,10 +666,10 @@
         ]
         + [
             vmem(NF, H, dtype=F32), vmem(NF, H), vmem(NF, H), vmem(GC, H), vmem(NG - 1, NC, H),
-            vmem(NC, H), vmem(GC, H), vmem(NC, H), vmem(GC, H), vmem(NF, H), vmem(NF, H, dtype=F32),
+            vmem(NC, H), vmem(GC, H), vmem(NC, H), vmem(GC, H), vmem(NF, H), vmem(NF, H), vmem(EF, H, dtype=F32), vmem(NF, H, dtype=F32),
             vmem(NT, H, dtype=F32), vmem(1024, H, dtype=F32), vmem(WROWS, H), vmem(EF, H), vmem(EF, H),
             vmem(256, H), vmem(256, H), vmem(8, H, dtype=F32), vmem(8, H, dtype=F32),
-            vmem(NG - 1, 8, H, dtype=F32), vmem(NR - 1, 8, H, dtype=F32),
+            vmem(NG, 8, H, dtype=F32), vmem(NR, 8, H, dtype=F32),
         ]
         + sems(*[1] * 16, 2 * blocks + 2)
         + Total.scratch(*EARLY)

time: 87.5 us -> 86.2 us (0.985)
  Pallas kernels: 86 us -> 84.5 us
    pallas_call x1, Pallas kernels: 77.7 us -> 76.2 us  [body(): pl.pallas_call(step_kernel, out_shape=[shape((WROWS, H)), shape((8, H), F...]
where the time goes in v5:
time: 86.2 us; the launch traced here: 86 us
  Pallas kernels  84.5 us (98%)
  between operations  1.47 us (2%)
    pallas_call x1, Pallas kernels, body(): pl.pallas_call(step_kernel, out_shape=[shape((WROWS, H)), shape((8, H), F...  76.2 us
    pallas_call x1, Pallas kernels, body(): pl.pallas_call(result_kernel, out_shape=[shape((H,), F32)] * 3 + [shape((...  8.25 us

profile of v5, /device:TPU:1, one launch (start us, length us, event | category | flops | bytes accessed | tf_op | source)
XLA Modules:
  0.0 86.0 jit_solution(3278546442464918547)
XLA Ops:
  1.3 76.2 %step.1 = (bf16[2560,256]{1,0:T(8,128)(2,1)}, f32[8,256]{1,0:T(8,128)}, f32[1024,256]{1,0:T(8,128)}, f32[1024,256]{1,0:T(8,128)}, bf16[4096,256]{1,0:T(8,128)(2,1)}, /*index=5*/bf16[4096,256]{1,0:T(8,128)(2,1)}) custom-call(s32[1]{0:T(128)S(6)} %copy.35.count, s32[8,32]{1,0:T(8,128)} %bitcast.8, s32[8,128]{1,0:T(8,128)} %bitcast.9, s32[32,128]{1,0:T(8,128)} %bitcast.6, ...), custom_call_target="tpu_custom_call" | custom-call | tf_op jit(solution)/shard_map/step/pallas_call | solution.py:649
  77.5 8.2 %results.1 = (f32[256]{0:T(256)}, f32[256]{0:T(256)}, f32[256]{0:T(256)}, f32[4096,256]{1,0:T(8,128)}, f32[4096,256]{1,0:T(8,128)}, /*index=5*/f32[1024,256]{1,0...) custom-call(f32[8,256]{1,0:T(8,128)} %get-tuple-element.34.b, ...), custom_call_target="tpu_custom_call" | custom-call | tf_op jit(solution)/shard_map/results/pallas_call | solution.py:685

commit v6 on v5

--- a/solution.py
+++ b/solution.py
@@ -277,25 +277,27 @@
     return wait
 
 
-def step_kernel(count, hidx, ct, snd, rcv, nf_h, gz_h, pw_h, ein_h, ef_h, ebias_h, eout_h, nin_h,
+def step_kernel(count, hidx_h, ct_h, snd_h, rcv_h, nf_h, gz_h, pw_h, ein_h, ef_h, ebias_h, eout_h, nin_h,
                 nbias_h, nout_h, rw_h, cin_h, cbias_h, cout_h, prol_h, ge_h,
-                w_out, b_out, nr_out, dn_out, def_out, en_out,
+                w_hbm, b_hbm, nr_out, dn_out, def_out, en_out,
+                hidx, ct, snd, rcv, small, w_out, b_out,
                 nf, gz, pw, ein, ef, ebias, eout, nin, nbias, nout, rw, cin, cbias, cout, prol, ge, ls,
                 own, halo, spart, sland, xs, xr, he, ds, enb, acc, agg,
                 y, hn, dsn, part, cland, gc_own, gc, q_own, q_all, gagg, gagg_w, gue0, gyn, ssum, wacc, wbuf, gueb_s,
                 defb, dh, hland, bias0, bias1, bl1, bl2,
                 fs, fr, sss, ssr, css, csr, cgs, cgr, qs, qr, hs, hr, c1s, c1r, c2s, c2r, outs, *sums):
     r, g = here()
-    ready = greet(r, g, ALL_PEERS)
     half_way = len(sums) // 2
     early = Total(r, g, wbuf, w_out, W_LATE, *EARLY, sums[:half_way])
     late = Total(r, g, wbuf, w_out, 0, *LATE, sums[half_way:])
+    indexed = fetch([(hidx_h, hidx), (ct_h, ct), (snd_h, snd), (rcv_h, rcv)], small)
     loaded = fetch(
         [(nf_h, nf), (gz_h, gz), (pw_h, pw), (ein_h, ein), (ef_h, ef), (ebias_h, ebias), (eout_h, eout),
          (nin_h, nin), (nbias_h, nbias), (nout_h, nout), (rw_h, rw), (cin_h, cin), (cbias_h, cbias),
          (cout_h, cout), (prol_h, prol), (ge_h, ge)],
         ls,
     )
+    ready = greet(r, g, ALL_PEERS)
     per = SUB // 128
 
     def grp(k):
@@ -335,6 +337,7 @@
         at = pl.ds(pl.multiple_of(step * BLK + h * SUB, SUB), SUB)
         return at, slice(h * per, (h + 1) * per), step * BLK + h * SUB
 
+    indexed(0)
     pick = halo_pick(hidx[...], 0, NF)
     loaded(0)
     own[...] = mm(pick, nf[...]).astype(BF)
@@ -342,6 +345,7 @@
     there = swap_halo(own, halo, fs, fr, 1)
     for c in there:
         c.start()
+    indexed(1, 2, 3)
     loaded(1, 2)
     spart[...] = mm(hot_rows(ct[...], 0, GC, pw[...].astype(F32)), gz[...]).astype(BF)
     scat_s = scatter_grp(r, g, spart, sland, sss, ssr, NC)
@@ -568,21 +572,31 @@
         total += bl2[k]
     b_out[...] = total
     early.finish()
+    keep_b = pltpu.make_async_copy(b_out, b_hbm, outs.at[last + 2])
+    keep_b.start()
+    early_rows, late_rows = pl.ds(W_LATE, W_EARLY), pl.ds(0, W_LATE)
+    keep_early = pltpu.make_async_copy(w_out.at[early_rows], w_hbm.at[early_rows], outs.at[last + 3])
+    keep_early.start()
     for step in range(EF // BLK):
         keep_en(step).wait()
         keep_def(step).wait()
     keep_nr.wait()
     keep_dn.wait()
     late.finish()
+    keep_late = pltpu.make_async_copy(w_out.at[late_rows], w_hbm.at[late_rows], outs.at[last + 4])
+    keep_late.start()
+    keep_b.wait()
+    keep_early.wait()
+    keep_late.wait()
 
 
 SIZES = (768, 256, 512, 256, 256, 256, 256)
 CHUNK = 2048
 
 
-def result_kernel(b, nr_h, dn_h, de_h, en_h, w_h, *refs):
+def result_kernel(b_h, nr_h, dn_h, de_h, en_h, w_h, *refs):
     biases, big, mats = refs[0:3], refs[3:7], refs[7:14]
-    nr, dn, de, en, w, wide_de, wide_en, wide_w, in_sem, out_sem = refs[14:]
+    nr, dn, de, en, w, wide_de, wide_en, wide_w, b, *lines, in_sem, out_sem = refs[14:]
     chunks = [pl.ds(c * CHUNK, CHUNK) for c in range(EF // CHUNK)]
     arriving, leaving = [], []
 
@@ -600,6 +614,7 @@
         for src, mid, wide, dst in ((en_h, en, wide_en, big[0]), (de_h, de, wide_de, big[1])):
             edges.append((bring(src.at[at], mid.at[at]), mid, wide, dst, at))
     nodes = [(bring(src, mid), mid, dst) for src, mid, dst in ((nr_h, nr, big[2]), (dn_h, dn, big[3]))]
+    b_here = bring(b_h, b)
     w_here = bring(w_h, w)
     for here_, mid, wide, dst, at in edges:
         here_.wait()
@@ -608,14 +623,16 @@
     for here_, mid, dst in nodes:
         here_.wait()
         leave(mid, dst)
+    b_here.wait()
+    for i, (line, dst) in enumerate(zip(lines, biases)):
+        line[...] = b[i : i + 1].reshape(H)
+        leave(line, dst)
     w_here.wait()
     first = 0
     for dst, size in zip(mats, SIZES):
         wide_w[first : first + size] = w[first : first + size].astype(F32)
         leave(wide_w.at[pl.ds(first, size)], dst)
         first += size
-    for i, dst in enumerate(biases):
-        dst[...] = b[i : i + 1].reshape(H)
     for c in leaving:
         c.wait()
 
@@ -636,9 +653,6 @@
     def sems(*sizes):
         return [pltpu.SemaphoreType.DMA((n,)) for n in sizes]
 
-    def whole(n):
-        return [pl.BlockSpec(memory_space=pltpu.VMEM)] * n
-
     def far(n):
         return [pl.BlockSpec(memory_space=pl.ANY)] * n
 
@@ -652,9 +666,15 @@
             shape((WROWS, H)), shape((8, H), F32), shape((NF, H), F32), shape((NF, H), F32),
             shape((EF, H)), shape((EF, H)),
         ],
-        in_specs=[pl.BlockSpec(memory_space=pltpu.SMEM)] + whole(4) + far(16),
-        out_specs=whole(2) + far(4),
+        in_specs=[pl.BlockSpec(memory_space=pltpu.SMEM)] + far(20),
+        out_specs=far(6),
         scratch_shapes=[
+            vmem(8, 32, dtype=I32), vmem(8, 128, dtype=I32), vmem(EF // 128, 128, dtype=I32),
+            vmem(EF // 128, 128, dtype=I32),
+        ]
+        + sems(4)
+        + [
+            vmem(WROWS, H), vmem(8, H, dtype=F32),
             vmem(NF, H), vmem(NF, H), vmem(8, 128), vmem(768, H), vmem(EF, H), vmem(H), vmem(H, H),
             vmem(512, H), vmem(H), vmem(H, H), vmem(8, 128), vmem(H, H), vmem(H), vmem(H, H), vmem(H, H),
             vmem(EF, H),
@@ -671,7 +691,7 @@
             vmem(256, H), vmem(256, H), vmem(8, H, dtype=F32), vmem(8, H, dtype=F32),
             vmem(NG, 8, H, dtype=F32), vmem(NR, 8, H, dtype=F32),
         ]
-        + sems(*[1] * 16, 2 * blocks + 2)
+        + sems(*[1] * 16, 2 * blocks + 5)
         + Total.scratch(*EARLY)
         + Total.scratch(*LATE),
         compiler_params=pltpu.CompilerParams(
@@ -685,13 +705,14 @@
     g_eb, g_nb, g_cb, edge_new, d_edge_feat, node_result, d_node_feat, *mats = pl.pallas_call(
         result_kernel,
         out_shape=[shape((H,), F32)] * 3 + [shape((n, H), F32) for n in (EF, EF, NF, NF) + SIZES],
-        in_specs=whole(1) + far(5),
-        out_specs=whole(3) + far(11),
+        in_specs=far(6),
+        out_specs=far(14),
         scratch_shapes=[
             vmem(NF, H, dtype=F32), vmem(NF, H, dtype=F32), vmem(EF, H), vmem(EF, H), vmem(WROWS, H),
             vmem(EF, H, dtype=F32), vmem(EF, H, dtype=F32), vmem(WROWS, H, dtype=F32),
+            vmem(8, H, dtype=F32), *[vmem(H, dtype=F32)] * 3,
         ]
-        + sems(2 * chunks + 3, 2 * chunks + 9),
+        + sems(2 * chunks + 4, 2 * chunks + 12),
         compiler_params=pltpu.CompilerParams(vmem_limit_bytes=LIMIT * MIB),
         name="results",
     )(b_all, nr, dn, de, en, w_all)

time: 86.2 us -> 84.3 us (0.978)
  Pallas kernels: 84.5 us -> 82.7 us
    pallas_call x1, Pallas kernels: 8.25 us -> 7.08 us  [body(): pl.pallas_call(result_kernel, out_shape=[shape((H,), F32)] * 3 + [shape((...]
where the time goes in v6:
time: 84.3 us; the launch traced here: 84.2 us
  Pallas kernels  82.7 us (98%)
  between operations  1.47 us (2%)
    pallas_call x1, Pallas kernels, body(): pl.pallas_call(step_kernel, out_shape=[shape((WROWS, H)), shape((8, H), F...  75.6 us
    pallas_call x1, Pallas kernels, body(): pl.pallas_call(result_kernel, out_shape=[shape((H,), F32)] * 3 + [shape((...  7.08 us

profile of v6, /device:TPU:1, one launch (start us, length us, event | category | flops | bytes accessed | tf_op | source)
XLA Modules:
  0.0 84.2 jit_solution(2589439393759375878)
XLA Ops:
  1.3 75.6 %step.1 = (bf16[2560,256]{1,0:T(8,128)(2,1)}, f32[8,256]{1,0:T(8,128)}, f32[1024,256]{1,0:T(8,128)}, f32[1024,256]{1,0:T(8,128)}, bf16[4096,256]{1,0:T(8,128)(2,1)}, /*index=5*/bf16[4096,256]{1,0:T(8,128)(2,1)}) custom-call(s32[1]{0:T(128)S(6)} %copy.35.count, s32[8,32]{1,0:T(8,128)} %bitcast.8, s32[8,128]{1,0:T(8,128)} %bitcast.9, s32[32,128]{1,0:T(8,128)} %bitcast.6, ...), custom_call_target="tpu_custom_call" | custom-call | tf_op jit(solution)/shard_map/step/pallas_call | solution.py:663
  76.9 7.1 %results.1 = (f32[256]{0:T(256)}, f32[256]{0:T(256)}, f32[256]{0:T(256)}, f32[4096,256]{1,0:T(8,128)}, f32[4096,256]{1,0:T(8,128)}, /*index=5*/f32[1024,256]{1,0...) custom-call(f32[8,256]{1,0:T(8,128)} %get-tuple-element.34.b_h, ...), custom_call_target="tpu_custom_call" | custom-call | tf_op jit(solution)/shard_map/results/pallas_call | solution.py:705
